TPU v7x, 32 devices: a whole 2x2x4 slice. The times are simulated.
32 devices in a mesh: seq: 4 (over y, x), fsdp: 8 (over z, core).
Axes of the slice: x: 2, y: 2, z: 4, core: 2. Of those that a mesh axis runs over, the one named last changes fastest.
Arguments:
- patches: bfloat16 [8, 1024, 1152], P('fsdp'), may hold values from -6 to 6
- counts: int32 [8, 4], P('fsdp'), may hold values from 1 to 253, as said below
- starts: int32 [8, 4], P('fsdp'), may hold values from 0 to 511, as said below
- embeds: bfloat16 [8, 512, 2048], P('fsdp', 'seq'), may hold values from -6 to 6
- route_ids: int32 [8, 512, 6], P('fsdp'), may hold values from 0 to 63, all different within a row; in each aligned block of 512 rows (0 to 511, 512 to 1023, ..., all dimensions but the last counted through in order) at most 64 rows name the same one
- route_weights: float32 [8, 512, 6], P('fsdp'), may hold values from 0.1 to 0.6
- vit_gain: float32 [1152], replicated, may hold values from 0.5 to 1.5
- vit_fc1: bfloat16 [1152, 4304], P('fsdp', 'seq'), may hold values from -0.1875 to 0.1875
- vit_fc2: bfloat16 [1152, 4304], P('fsdp', 'seq'), may hold values from -0.09375 to 0.09375
- proj_gain: float32 [4608], replicated, may hold values from 0.5 to 1.5
- proj_weight: bfloat16 [4608, 2048], P('fsdp', 'seq'), may hold values from -0.09375 to 0.09375
- moe_gain: float32 [2048], replicated, may hold values from 0.5 to 1.5
- shared_gate: bfloat16 [2048, 2816], P('fsdp', 'seq'), may hold values from -0.125 to 0.125
- shared_up: bfloat16 [2048, 2816], P('fsdp', 'seq'), may hold values from -0.125 to 0.125
- shared_down: bfloat16 [2048, 2816], P('fsdp', 'seq'), may hold values from -0.109375 to 0.109375
- expert_gate: bfloat16 [2048, 4, 1408], P('fsdp', 'seq'), may hold values from -0.125 to 0.125
- expert_up: bfloat16 [2048, 4, 1408], P('fsdp', 'seq'), may hold values from -0.125 to 0.125
- expert_down: bfloat16 [2048, 4, 1408], P('fsdp', 'seq'), may hold values from -0.15625 to 0.15625
Outputs:
- layer_out: bfloat16 [8, 512, 2048], P('fsdp', 'seq')
Inputs may be any that keep to these rules, and one draw needn't show every extreme that they name: Per stream the counts of its 4 images sum to 256. `starts`: images of a stream lie in order in disjoint runs of positions inside its 512 positions; in each stream the 128 positions of some one index of seq are all visual. `route_ids`: the 6 experts of a token differ; in each stream no expert is chosen by more than 64 tokens.
All inputs are finite; a program needn't handle non-finite values.
Results may differ from a plain program's by a relative error of at most 0.014.
Values may be sent and summed in bfloat16 or wider, within the bound.
A program may use at most 128 MiB of HBM per device.

v0:
```python
import jax
import jax.numpy as jnp
from jax import lax
from jax.sharding import PartitionSpec as P

ln_epsilon = 1e-05
rms_epsilon = 1e-06


def layer_norm(values, gain_vec):
    center = values - jnp.mean(values, axis=-1, keepdims=True)
    spread = jnp.mean(center * center, axis=-1, keepdims=True)
    return center * lax.rsqrt(spread + ln_epsilon) * gain_vec


def rms_norm(values, gain_vec):
    square = jnp.mean(values * values, axis=-1, keepdims=True)
    return values * lax.rsqrt(square + rms_epsilon) * gain_vec


def visual_positions(counts, starts, total):
    end_index = jnp.cumsum(counts)
    begins = end_index - counts
    token_index = jnp.arange(total, dtype=jnp.int32)
    inside = (token_index[:, None] >= begins[None, :]) & (token_index[:, None] < end_index[None, :])
    placed = starts[None, :] + token_index[:, None] - begins[None, :]
    return jnp.sum(jnp.where(inside, placed, 0), axis=1)


def routed_rows(gathered, route_ids, route_weights, expert, capacity, gate_w, up_w, down_w):
    hit_mask = route_ids == expert
    chosen = jnp.any(hit_mask, axis=1)
    weight_sum = jnp.sum(jnp.where(hit_mask, route_weights, 0.0), axis=1)
    count_rows = gathered.shape[0]
    slot_rank = jnp.cumsum(chosen.astype(jnp.int32)) - 1
    target = jnp.where(chosen, slot_rank, capacity)
    slot_rows = (
        jnp.zeros((capacity,), jnp.int32)
        .at[target]
        .set(jnp.arange(count_rows, dtype=jnp.int32), mode="drop")
    )
    is_live = jnp.arange(capacity, dtype=jnp.int32) < jnp.sum(chosen.astype(jnp.int32))
    picked = jnp.take(gathered, slot_rows, axis=0)
    gate_part = jnp.dot(picked, gate_w, preferred_element_type=jnp.float32)
    up_part = jnp.dot(picked, up_w, preferred_element_type=jnp.float32)
    hidden = (jax.nn.silu(gate_part) * up_part).astype(jnp.bfloat16)
    result = lax.dot_general(
        hidden, down_w, (((1,), (1,)), ((), ())), preferred_element_type=jnp.float32
    )
    factor = jnp.where(is_live, jnp.take(weight_sum, slot_rows), 0.0)
    return (slot_rows, result * factor[:, None])


def shards(
    patches,
    counts,
    starts,
    embeds,
    route_ids,
    route_weights,
    vit_gain,
    vit_fc1,
    vit_fc2,
    proj_gain,
    proj_weight,
    moe_gain,
    shared_gate,
    shared_up,
    shared_down,
    expert_gate,
    expert_up,
    expert_down,
):
    seq_count = lax.axis_size("seq")
    seq_index = lax.axis_index("seq")
    vit_first, vit_second, projector = (
        lax.all_gather(vit_fc1, "fsdp", axis=0, tiled=True),
        lax.all_gather(vit_fc2, "fsdp", axis=0, tiled=True),
        lax.all_gather(proj_weight, "fsdp", axis=0, tiled=True),
    )
    image_rows = patches[0].astype(jnp.float32)
    normed = layer_norm(image_rows, vit_gain).astype(jnp.bfloat16)
    hidden = jax.nn.gelu(
        jnp.dot(normed, vit_first, preferred_element_type=jnp.float32), approximate=True
    ).astype(jnp.bfloat16)
    product = lax.dot_general(
        hidden, vit_second, (((1,), (1,)), ((), ())), preferred_element_type=jnp.float32
    )
    mixed_sum = lax.psum(product.astype(jnp.bfloat16), "seq").astype(jnp.float32)
    residual = image_rows + mixed_sum
    joined_width = residual.shape[1] * 4
    proj_in = layer_norm(residual.reshape(-1, joined_width), proj_gain).astype(jnp.bfloat16)
    visual = jnp.dot(proj_in, projector, preferred_element_type=jnp.float32).astype(jnp.bfloat16)
    tok_dev = embeds.shape[1]
    positions = visual_positions(counts[0], starts[0], visual.shape[0])
    owners = positions // tok_dev
    one_hot = (owners[:, None] == jnp.arange(seq_count, dtype=jnp.int32)[None, :]).astype(jnp.int32)
    slot_rank = jnp.sum((jnp.cumsum(one_hot, axis=0) - one_hot) * one_hot, axis=1)
    slot_index = owners * tok_dev + slot_rank
    send_buffer = (
        jnp.zeros((seq_count * tok_dev, visual.shape[1]), jnp.bfloat16).at[slot_index].set(visual)
    )
    received = lax.all_to_all(
        send_buffer.reshape(seq_count, tok_dev, visual.shape[1]),
        "seq",
        split_axis=0,
        concat_axis=2,
        tiled=True,
    )
    is_mine = owners == seq_index
    local_rows = positions % tok_dev
    slot_place = (
        jnp.full((tok_dev,), tok_dev, jnp.int32)
        .at[jnp.where(is_mine, slot_rank, tok_dev)]
        .set(local_rows, mode="drop")
    )
    merged = embeds[0].at[slot_place].set(received[0], mode="drop")
    normed_tokens = rms_norm(merged.astype(jnp.float32), moe_gain).astype(jnp.bfloat16)
    gathered = lax.all_gather(normed_tokens, "seq", axis=0, tiled=True)
    gate_shared, up_shared, down_shared, gate_expert, up_expert, down_expert = (
        lax.all_gather(shared_gate, "fsdp", axis=0, tiled=True),
        lax.all_gather(shared_up, "fsdp", axis=0, tiled=True),
        lax.all_gather(shared_down, "fsdp", axis=0, tiled=True),
        lax.all_gather(expert_gate, "fsdp", axis=0, tiled=True),
        lax.all_gather(expert_up, "fsdp", axis=0, tiled=True),
        lax.all_gather(expert_down, "fsdp", axis=0, tiled=True),
    )
    gate_part = jnp.dot(gathered, gate_shared, preferred_element_type=jnp.float32)
    up_part = jnp.dot(gathered, up_shared, preferred_element_type=jnp.float32)
    shared_hidden = (jax.nn.silu(gate_part) * up_part).astype(jnp.bfloat16)
    partial_value = lax.dot_general(
        shared_hidden, down_shared, (((1,), (1,)), ((), ())), preferred_element_type=jnp.float32
    )
    capacity = gathered.shape[0] // 8
    local_count = gate_expert.shape[1]
    expert = seq_index * local_count + 0
    slot_rows, values = routed_rows(
        gathered,
        route_ids[0],
        route_weights[0],
        expert,
        capacity,
        gate_expert[:, 0, :],
        up_expert[:, 0, :],
        down_expert[:, 0, :],
    )
    partial_value = partial_value.at[slot_rows].add(values)
    summed = lax.psum_scatter(
        partial_value.astype(jnp.bfloat16), "seq", scatter_dimension=0, tiled=True
    ).astype(jnp.float32)
    layer_out = (merged.astype(jnp.float32) + summed).astype(jnp.bfloat16)
    return layer_out[None]


def solution(mesh):
    placed = (
        P("fsdp", None, None),
        P("fsdp", None),
        P("fsdp", None),
        P("fsdp", "seq", None),
        P("fsdp", None, None),
        P("fsdp", None, None),
        P(),
        P("fsdp", "seq"),
        P("fsdp", "seq"),
        P(),
        P("fsdp", "seq"),
        P(),
        P("fsdp", "seq"),
        P("fsdp", "seq"),
        P("fsdp", "seq"),
        P("fsdp", "seq", None),
        P("fsdp", "seq", None),
        P("fsdp", "seq", None),
    )
    return jax.shard_map(
        shards, mesh=mesh, in_specs=placed, out_specs=P("fsdp", "seq", None), check_vma=False
    )
```

profile of v0, /device:TPU:0, one launch (start us, length us, event | category | flops | bytes accessed | tf_op | source)
XLA Modules:
  0.0 629.4 jit_solution(5664289098593353757)
XLA Ops:
  10.9 35.0 %all-gather.11.cloned.1.call-done = bf16[1152,1076]{1,0:T(8,128)(2,1)} async-done(((bf16[144,1076]{1,0:T(8,128)(2,1)}), bf16[1152,1076]{1,0:T(8,128)(2,1)}) %all-gather.11.cloned.1.call-update) | async-done | bytes 2479120 | tf_op jit(solution)/shard_map/all_gather | solution.py:77
  45.9 34.8 %all-gather.13.cloned.1.call-done = bf16[1152,1076]{1,0:T(8,128)(2,1)} async-done(((bf16[144,1076]{1,0:T(8,128)(2,1)}), bf16[1152,1076]{1,0:T(8,128)(2,1)}) %all-gather.13.cloned.1.call-update) | async-done | bytes 2479120 | tf_op jit(solution)/shard_map/all_gather | solution.py:78
  80.7 11.6 %convolution_convert_fusion = bf16[1024,1152]{1,0:T(8,128)(2,1)} fusion(bf16[1152,1076]{1,0:T(8,128)(2,1)} %all-gather.13.cloned.1.call-done, bf16[1152,1076]{1,0:T(8,128)(2,1)} %all-gather.11.cloned.1.call-done, bf16[1,1024,1152]{2,1,0:T(8,128)(2,1)S(1)} %copy-done.1, f32[1152]{0:T(1024)S(1)} %copy-done.8, f32[1024]{0:T(1024)S(1)} %add_rsqrt_fusion, ...), kind=kOutput, calls=%fused_computation.33 | convolution fusion | flops 5094199296 | bytes 9689600 | tf_op jit(solution)/shard_map/dot_general | solution.py:86
  94.9 70.6 %all-reduce.2.cloned.1.call-done = bf16[1024,1152]{1,0:T(8,128)(2,1)} async-done(((bf16[1024,1152]{1,0:T(8,128)(2,1)}), bf16[1024,1152]{1,0:T(8,128)(2,1)}) %all-reduce.2.cloned.1.call-update) | async-done | bytes 2359312 | tf_op jit(solution)/shard_map/psum | solution.py:89
  168.4 4.8 multiply_reduce_fusion
  173.1 5.5 reshape.238
  178.9 40.0 %all-gather.15.cloned.1.call-done = bf16[4608,512]{1,0:T(8,128)(2,1)} async-done(((bf16[576,512]{1,0:T(8,128)(2,1)}), bf16[4608,512]{1,0:T(8,128)(2,1)}) %all-gather.15.cloned.1.call-update) | async-done | bytes 4718608 | tf_op jit(solution)/shard_map/all_gather | solution.py:79
  218.9 5.2 fusion.42
  226.4 3.7 all-to-all-start
  231.5 7.1 %all-to-all-done = bf16[4,128,512]{2,1,0:T(8,128)(2,1)S(1)} async-done(((bf16[4,128,512]{2,1,0:T(8,128)(2,1)}), bf16[4,128,512]{2,1,0:T(8,128)(2,1)S(1)}, u32[]{:S(2)}, u32[]{:S(2)}) %all-to-all-start) | async-done | bytes 524320 | tf_op jit(solution)/shard_map/all_to_all | solution.py:103
  251.8 23.6 %all-gather.17.cloned.1.call-done = bf16[512,2048]{1,0:T(8,128)(2,1)} async-done(((bf16[128,2048]{1,0:T(8,128)(2,1)}), bf16[512,2048]{1,0:T(8,128)(2,1)}) %all-gather.17.cloned.1.call-update) | async-done | bytes 2097168 | tf_op jit(solution)/shard_map/all_gather | solution.py:119
  278.4 59.0 %all-gather.25.cloned.1.call-done = bf16[2048,1,1408]{2,0,1:T(8,128)(2,1)} async-done(((bf16[256,1,1408]{2,0,1:T(8,128)(2,1)}), bf16[2048,1,1408]{2,0,1:T(8,128)(2,1)}) %all-gather.25.cloned.1.call-update) | async-done | bytes 5767184 | tf_op jit(solution)/shard_map/all_gather | solution.py:124
  337.4 3.8 fusion.6
  341.2 33.6 %all-gather.19.cloned.1.call-done = bf16[2048,704]{0,1:T(8,128)(2,1)} async-done(((bf16[256,704]{0,1:T(8,128)(2,1)}), bf16[2048,704]{0,1:T(8,128)(2,1)}) %all-gather.19.cloned.1.call-update) | async-done | bytes 2883600 | tf_op jit(solution)/shard_map/all_gather | solution.py:121
  374.8 4.6 fusion.81
  379.4 32.4 %all-gather.21.cloned.1.call-done = bf16[2048,704]{0,1:T(8,128)(2,1)} async-done(((bf16[256,704]{0,1:T(8,128)(2,1)}), bf16[2048,704]{0,1:T(8,128)(2,1)}) %all-gather.21.cloned.1.call-update) | async-done | bytes 2883600 | tf_op jit(solution)/shard_map/all_gather | solution.py:122
  411.8 37.0 %all-gather.23.cloned.1.call-done = bf16[2048,704]{0,1:T(8,128)(2,1)} async-done(((bf16[256,704]{0,1:T(8,128)(2,1)}), bf16[2048,704]{0,1:T(8,128)(2,1)}) %all-gather.23.cloned.1.call-update) | async-done | bytes 2883600 | tf_op jit(solution)/shard_map/all_gather | solution.py:123
  448.8 8.6 %fusion.49 = f32[512,2048]{1,0:T(8,128)} fusion(bf16[2048,704]{0,1:T(8,128)(2,1)} %all-gather.23.cloned.1.call-done, bf16[512,2048]{1,0:T(8,128)(2,1)S(1)} %copy-done.2, bf16[2048,704]{0,1:T(8,128)(2,1)} %all-gather.21.cloned.1.call-done, f32[512,704]{0,1:T(8,128)} %fusion.81), kind=kOutput, calls=%fused_computation.55 | convolution fusion | flops 2954952704 | bytes 13500416 | tf_op jit(solution)/shard_map/dot_general | solution.py:131
  457.4 51.7 %all-gather.27.cloned.1.call-done = bf16[2048,1,1408]{2,0,1:T(8,128)(2,1)} async-done(((bf16[256,1,1408]{2,0,1:T(8,128)(2,1)}), bf16[2048,1,1408]{2,0,1:T(8,128)(2,1)}) %all-gather.27.cloned.1.call-update) | async-done | bytes 5767184 | tf_op jit(solution)/shard_map/all_gather | solution.py:125
  509.0 60.9 %all-gather.29.cloned.1.call-done = bf16[2048,1,1408]{2,0,1:T(8,128)(2,1)} async-done(((bf16[256,1,1408]{2,0,1:T(8,128)(2,1)}), bf16[2048,1,1408]{2,0,1:T(8,128)(2,1)}) %all-gather.29.cloned.1.call-update) | async-done | bytes 5767184 | tf_op jit(solution)/shard_map/all_gather | solution.py:126
  569.9 7.2 %fusion.35 = f32[64,2048]{1,0:T(8,128)S(1)} fusion(bf16[2048,1,1408]{2,0,1:T(8,128)(2,1)} %all-gather.29.cloned.1.call-done, bf16[2048,1,1408]{2,0,1:T(8,128)(2,1)} %all-gather.27.cloned.1.call-done, f32[64,1408]{1,0:T(8,128)S(1)} %fusion.6, f32[64]{0:T(128)S(1)} %get-tuple-element.5, bf16[64,2048]{1,0:T(8,128)(2,1)S(1)} %gather_fusion, ...), kind=kOutput, calls=%fused_computation.43 | convolution fusion | flops 739000320 | bytes 12681536 | tf_op jit(solution)/shard_map/dot_general | solution.py:47
  577.2 5.5 scatter_fusion.1
  582.7 3.9 convert_element_type.80
  586.6 34.0 %reduce-scatter.2.cloned.1.call-done = bf16[128,2048]{1,0:T(8,128)(2,1)} async-done(((bf16[512,2048]{1,0:T(8,128)(2,1)}), bf16[128,2048]{1,0:T(8,128)(2,1)}) %reduce-scatter.2.cloned.1.call-update) | async-done | bytes 524304 | tf_op jit(solution)/shard_map/reduce_scatter | solution.py:148
  (100 shorter events, 31.6 us)
Async XLA Ops:
  6.5 3.6 copy-start.1
  6.5 74.2 %copy-start.8 = (f32[1152]{0:T(1024)S(1)}, f32[1152]{0:T(1024)}, u32[]{:S(2)}) copy-start(f32[1152]{0:T(1024)} %param.24) | copy-start | bytes 13828
  6.5 39.4 %all-gather.11.cloned.1.call-start = ((), (), s32[]{:S(2)}) async-start(), calls=%async_computation.2 | async-start | bytes 2985984 | tf_op jit(solution)/shard_map/all_gather | solution.py:77
  7.3 73.4 %all-gather.13.cloned.1.call-start = ((), (), s32[]{:S(2)}) async-start(), calls=%async_computation.3 | async-start | bytes 2985984 | tf_op jit(solution)/shard_map/all_gather | solution.py:78
  8.0 157.5 %all-reduce.2.cloned.1.call-start = ((), (), s32[]{:S(2)}) async-start(), calls=%async_computation.4 | async-start | bytes 4718592 | tf_op jit(solution)/shard_map/psum | solution.py:89
  10.9 82.0 %copy-start.9 = (s32[1,4]{1,0:T(1,128)S(1)}, s32[1,4]{1,0:T(1,128)}, u32[]{:S(2)}) copy-start(s32[1,4]{1,0:T(1,128)} %param.19) | copy-start | bytes 52
  10.9 82.2 %copy-start.6 = (s32[1,4]{1,0:T(1,128)S(1)}, s32[1,4]{1,0:T(1,128)}, u32[]{:S(2)}) copy-start(s32[1,4]{1,0:T(1,128)} %param.20) | copy-start | bytes 52
  92.4 126.5 %all-gather.15.cloned.1.call-start = ((), (), s32[]{:S(2)}) async-start(), calls=%async_computation.5 | async-start | bytes 5308416 | tf_op jit(solution)/shard_map/all_gather | solution.py:79
  173.1 45.7 %copy-start.7 = (f32[4608]{0:T(1024)S(1)}, f32[4608]{0:T(1024)}, u32[]{:S(2)}) copy-start(f32[4608]{0:T(1024)} %param.27) | copy-start | bytes 55300
  224.1 15.0 %copy-start = (bf16[1,128,2048]{2,1,0:T(8,128)(2,1)S(1)}, bf16[1,128,2048]{2,1,0:T(8,128)(2,1)}, u32[]{:S(2)}) copy-start(bf16[1,128,2048]{2,1,0:T(8,128)(2,1)} %param.21) | copy-start | bytes 1572868
  226.4 12.1 %all-to-all-start = ((bf16[4,128,512]{2,1,0:T(8,128)(2,1)}), bf16[4,128,512]{2,1,0:T(8,128)(2,1)S(1)}, u32[]{:S(2)}, u32[]{:S(2)}) async-start(bf16[4,128,512]{2,1,0:T(8,128)(2,1)} %bitcast.14), calls=%async_computation | async-start | bytes 1048576 | tf_op jit(solution)/shard_map/all_to_all | solution.py:103
  230.1 45.3 %all-gather.17.cloned.1.call-start = ((), (), s32[]{:S(2)}) async-start(), calls=%async_computation.6 | async-start | bytes 2621440 | tf_op jit(solution)/shard_map/all_gather | solution.py:119
  239.1 1.9 copy-start.5
  240.8 5.4 copy-start.3
  240.8 8.8 %copy-start.4 = (f32[1,512,6]{1,0,2:T(1,128)S(1)}, f32[1,512,6]{1,0,2:T(1,128)}, u32[]{:S(2)}) copy-start(f32[1,512,6]{1,0,2:T(1,128)} %param.23) | copy-start | bytes 36868
  242.0 95.4 %all-gather.25.cloned.1.call-start = ((), (), s32[]{:S(2)}) async-start(), calls=%async_computation.10 | async-start | bytes 6488064 | tf_op jit(solution)/shard_map/all_gather | solution.py:124
  242.6 132.3 %all-gather.19.cloned.1.call-start = ((), (), s32[]{:S(2)}) async-start(), calls=%async_computation.7 | async-start | bytes 3244032 | tf_op jit(solution)/shard_map/all_gather | solution.py:121
  243.3 168.5 %all-gather.21.cloned.1.call-start = ((), (), s32[]{:S(2)}) async-start(), calls=%async_computation.8 | async-start | bytes 3244032 | tf_op jit(solution)/shard_map/all_gather | solution.py:122
  244.1 204.7 %all-gather.23.cloned.1.call-start = ((), (), s32[]{:S(2)}) async-start(), calls=%async_computation.9 | async-start | bytes 3244032 | tf_op jit(solution)/shard_map/all_gather | solution.py:123
  244.8 264.2 %all-gather.27.cloned.1.call-start = ((), (), s32[]{:S(2)}) async-start(), calls=%async_computation.11 | async-start | bytes 6488064 | tf_op jit(solution)/shard_map/all_gather | solution.py:125
  245.4 324.5 %all-gather.29.cloned.1.call-start = ((), (), s32[]{:S(2)}) async-start(), calls=%async_computation.12 | async-start | bytes 6488064 | tf_op jit(solution)/shard_map/all_gather | solution.py:126
  246.1 374.5 %reduce-scatter.2.cloned.1.call-start = ((), (), s32[]{:S(2)}) async-start(), calls=%async_computation.13 | async-start | bytes 2621440 | tf_op jit(solution)/shard_map/reduce_scatter | solution.py:148
  275.4 99.5 %copy-start.2 = (bf16[512,2048]{1,0:T(8,128)(2,1)S(1)}, bf16[512,2048]{1,0:T(8,128)(2,1)}, u32[]{:S(2)}) copy-start(bf16[512,2048]{1,0:T(8,128)(2,1)} %all-gather.17.cloned.1.call-done) | copy-start | bytes 6291460
Sparse Core Ops, SparseCore 0:
  9.0 36.8 all-gather.10
  47.5 33.1 all-gather.12
  92.5 73.0 all-reduce.1
  167.1 51.6 all-gather.14
  242.1 33.1 all-gather.16
  276.9 60.4 all-gather.24
  339.1 35.7 all-gather.18
  376.5 35.2 all-gather.20
  413.5 35.2 all-gather.22
  450.3 58.6 all-gather.26
  510.8 59.0 all-gather.28
  586.7 33.8 reduce-scatter.1
where the time goes:
time: 630 us; the launch traced here: 629 us
  waiting for transfers between devices  525 us (83%)
  matrix products  41.1 us (7%)
  other arithmetic  26.3 us (4%)
  local copies, waits for them, and re-layouts  18.8 us (3%)
  between operations  13.8 us (2%)
    psum x1, waiting for transfers between devices, shards(): lax.psum(product.astype(jnp.bfloat16), 'seq').astype(jnp.float32)  70.6 us
    all_gather x1, waiting for transfers between devices, shards(): lax.all_gather(expert_down, 'fsdp', axis=0, tiled=True)  60.9 us
    all_gather x1, waiting for transfers between devices, shards(): lax.all_gather(expert_gate, 'fsdp', axis=0, tiled=True)  59 us
    all_gather x1, waiting for transfers between devices, shards(): lax.all_gather(expert_up, 'fsdp', axis=0, tiled=True)  51.7 us
    all_gather x1, waiting for transfers between devices, shards(): lax.all_gather(proj_weight, 'fsdp', axis=0, tiled=True)  40 us
    all_gather x1, waiting for transfers between devices, shards(): lax.all_gather(shared_down, 'fsdp', axis=0, tiled=True)  37 us
    all_gather x1, waiting for transfers between devices, shards(): lax.all_gather(vit_fc1, 'fsdp', axis=0, tiled=True)  35 us
    all_gather x1, waiting for transfers between devices, shards(): lax.all_gather(vit_fc2, 'fsdp', axis=0, tiled=True)  34.8 us
  transfers between devices with their start and end apart: 13, of which 13 were waited for; matrix products, arithmetic and copies ran while one was open for 7% of the time, Pallas kernels for 0%

commit v1 on v0

v1 whole, which is shorter than its diff:
```python
import jax
import jax.numpy as jnp
from jax import lax
from jax.sharding import PartitionSpec as P

ln_epsilon = 1e-05
rms_epsilon = 1e-06
bf16 = jnp.bfloat16
f32 = jnp.float32


def layer_norm(values, gain_vec):
    center = values - jnp.mean(values, axis=-1, keepdims=True)
    spread = jnp.mean(center * center, axis=-1, keepdims=True)
    return center * lax.rsqrt(spread + ln_epsilon) * gain_vec


def rms_norm(values, gain_vec):
    square = jnp.mean(values * values, axis=-1, keepdims=True)
    return values * lax.rsqrt(square + rms_epsilon) * gain_vec


def visual_positions(counts, starts, total):
    images = jnp.arange(counts.shape[0], dtype=jnp.int32)
    end_index = jnp.sum(jnp.where(images[None, :] <= images[:, None], counts[None, :], 0), axis=1)
    begins = end_index - counts
    token_index = jnp.arange(total, dtype=jnp.int32)
    inside = (token_index[:, None] >= begins[None, :]) & (token_index[:, None] < end_index[None, :])
    placed = starts[None, :] + token_index[:, None] - begins[None, :]
    return jnp.sum(jnp.where(inside, placed, 0), axis=1)


def exchange(blocks, axis):
    return lax.all_to_all(blocks, axis, split_axis=0, concat_axis=0, tiled=True)


def spread_blocks(block, axis, count):
    return exchange(jnp.broadcast_to(block[None], (count,) + block.shape), axis)


def dot_t(left, right):
    return lax.dot_general(left, right, (((1,), (1,)), ((), ())), preferred_element_type=f32)


def dot(left, right):
    return jnp.dot(left, right, preferred_element_type=f32)


def shards(
    patches,
    counts,
    starts,
    embeds,
    route_ids,
    route_weights,
    vit_gain,
    vit_fc1,
    vit_fc2,
    proj_gain,
    proj_weight,
    moe_gain,
    shared_gate,
    shared_up,
    shared_down,
    expert_gate,
    expert_up,
    expert_down,
):
    n_seq = lax.axis_size("seq")
    me = lax.axis_index("seq")
    n_fsdp = lax.axis_size("fsdp")

    vit_first = lax.all_gather(vit_fc1, "fsdp", axis=0, tiled=True)
    vit_fc2, vit_first = lax.optimization_barrier((vit_fc2, vit_first))
    vit_second = lax.all_gather(vit_fc2, "fsdp", axis=0, tiled=True)
    proj_weight, vit_second = lax.optimization_barrier((proj_weight, vit_second))
    projector = lax.all_gather(proj_weight, "fsdp", axis=0, tiled=True)
    shared_gate, projector = lax.optimization_barrier((shared_gate, projector))
    gate_shared = lax.all_gather(shared_gate, "fsdp", axis=0, tiled=True)
    shared_up, gate_shared = lax.optimization_barrier((shared_up, gate_shared))
    up_shared = lax.all_gather(shared_up, "fsdp", axis=0, tiled=True)
    shared_down, up_shared = lax.optimization_barrier((shared_down, up_shared))
    down_shared = lax.all_gather(shared_down, "fsdp", axis=0, tiled=True)

    width = embeds.shape[2]
    tok_dev = embeds.shape[1]
    all_embeds = spread_blocks(embeds[0], "seq", n_seq).reshape(n_seq * tok_dev, width)
    n_tok = n_seq * tok_dev

    rows = patches.shape[1]
    my_rows = rows // n_seq
    normed = layer_norm(patches[0].astype(f32), vit_gain).astype(bf16)
    hidden = jax.nn.gelu(dot(normed, vit_first), approximate=True).astype(bf16)
    product = dot_t(hidden, vit_second).astype(bf16)
    blocks = exchange(product.reshape(n_seq, my_rows, product.shape[1]), "seq")
    mixed = jnp.sum(blocks.astype(f32), axis=0)
    mine = lax.dynamic_slice_in_dim(patches[0], me * my_rows, my_rows, axis=0)
    residual = mine.astype(f32) + mixed

    joined = residual.shape[1] * 4
    proj_part = layer_norm(residual.reshape(-1, joined), proj_gain).astype(bf16)
    proj_in = spread_blocks(proj_part, "seq", n_seq).reshape(-1, joined)
    visual_part = dot(proj_in, projector).astype(bf16)
    n_vis = visual_part.shape[0]
    visual = spread_blocks(visual_part, "seq", n_seq).transpose(1, 0, 2).reshape(n_vis, width)

    positions = visual_positions(counts[0], starts[0], n_vis)
    token_ids = jnp.arange(n_tok, dtype=jnp.int32)
    place = positions[None, :] == token_ids[:, None]
    is_visual = jnp.any(place, axis=1)
    placed_visual = dot(place.astype(bf16), visual).astype(bf16)
    merged = jnp.where(is_visual[:, None], placed_visual, all_embeds)
    tokens = rms_norm(merged.astype(f32), moe_gain).astype(bf16)

    capacity = n_tok // 8
    hit_mask = route_ids[0] == me
    chosen = jnp.any(hit_mask, axis=1)
    weight_sum = jnp.sum(jnp.where(hit_mask, route_weights[0], 0.0), axis=1)
    before = (token_ids[None, :] < token_ids[:, None]) & chosen[None, :]
    rank = jnp.sum(before.astype(f32), axis=1).astype(jnp.int32)
    slot_ids = jnp.arange(capacity, dtype=jnp.int32)
    pick = chosen[None, :] & (rank[None, :] == slot_ids[:, None])
    picked = dot(pick.astype(bf16), tokens).astype(bf16)
    depth = expert_gate.shape[0]
    hid = expert_gate.shape[2]
    picked_cols = exchange(picked.reshape(capacity, n_fsdp, depth).transpose(1, 0, 2), "fsdp")
    picked_cols = picked_cols.reshape(n_fsdp * capacity, depth)
    gate_up = jnp.concatenate(
        [dot(picked_cols, expert_gate[:, 0, :]), dot(picked_cols, expert_up[:, 0, :])], axis=1
    ).astype(bf16)
    sums = jnp.sum(exchange(gate_up.reshape(n_fsdp, capacity, 2 * hid), "fsdp").astype(f32), axis=0)
    expert_hidden = (jax.nn.silu(sums[:, :hid]) * sums[:, hid:]).astype(bf16)
    all_hidden = spread_blocks(expert_hidden, "fsdp", n_fsdp).reshape(n_fsdp * capacity, hid)
    down_cols = dot_t(all_hidden, expert_down[:, 0, :]).astype(bf16)
    values = exchange(down_cols.reshape(n_fsdp, capacity, depth), "fsdp")
    values = values.transpose(1, 0, 2).reshape(capacity, width)
    routed = lax.dot_general(
        pick.astype(bf16), values, (((0,), (0,)), ((), ())), preferred_element_type=f32
    )

    shared_hidden = (jax.nn.silu(dot(tokens, gate_shared)) * dot(tokens, up_shared)).astype(bf16)
    partial_value = (dot_t(shared_hidden, down_shared) + routed * weight_sum[:, None]).astype(bf16)
    terms = exchange(partial_value.reshape(n_seq, tok_dev, width), "seq")
    summed = jnp.sum(terms.astype(f32), axis=0)
    own = lax.dynamic_slice_in_dim(merged, me * tok_dev, tok_dev, axis=0)
    return (own.astype(f32) + summed).astype(bf16)[None]


def solution(mesh):
    placed = (
        P("fsdp", None, None),
        P("fsdp", None),
        P("fsdp", None),
        P("fsdp", "seq", None),
        P("fsdp", None, None),
        P("fsdp", None, None),
        P(),
        P("fsdp", "seq"),
        P("fsdp", "seq"),
        P(),
        P("fsdp", "seq"),
        P(),
        P("fsdp", "seq"),
        P("fsdp", "seq"),
        P("fsdp", "seq"),
        P("fsdp", "seq", None),
        P("fsdp", "seq", None),
        P("fsdp", "seq", None),
    )
    return jax.shard_map(
        shards, mesh=mesh, in_specs=placed, out_specs=P("fsdp", "seq", None), check_vma=False
    )
```

time: 630 us -> 457 us (0.73)
  waiting for transfers between devices: 525 us -> 339 us
  starting transfers between devices: 4.23 us -> 35 us
  other arithmetic: 26.3 us -> 17.6 us
  local copies, waits for them, and re-layouts: 18.8 us -> 10.6 us
    all_gather x10 -> x6, waiting for transfers between devices: 408 us -> 116 us  [the longest x1 42.1 us: shards(): up_shared = lax.all_gather(shared_up, 'fsdp', axis=0, tiled=True)]
    all_to_all x1 -> x9, waiting for transfers between devices: 7.07 us -> 221 us  [exchange(): return lax.all_to_all(blocks, axis, split_axis=0, concat_axis=0, tiled=True)]
    psum x1 -> x0, waiting for transfers between devices: 70.6 us -> none  [shards(): lax.psum(product.astype(jnp.bfloat16), 'seq').astype(jnp.float32)]
    reduce_scatter x1 -> x0, waiting for transfers between devices: 34 us -> none  [shards(): lax.psum_scatter(partial_value.astype(jnp.bfloat16), 'seq', scatter_dimen...]
    all_to_all x1 -> x9, starting transfers between devices: 3.65 us -> 34.8 us  [exchange(): return lax.all_to_all(blocks, axis, split_axis=0, concat_axis=0, tiled=True)]
    scatter x4 -> x0, local copies, waits for them, and re-layouts: 7.99 us -> none  [the longest x1 2.66 us: routed_rows(): slot_rows = jnp.zeros((capacity,), jnp.int32).at[target].set(jnp.arange(c...]
    broadcast_in_dim x0 -> x4, local copies, waits for them, and re-layouts: none -> 6.54 us  [spread_blocks(): return exchange(jnp.broadcast_to(block[None], (count,) + block.shape), axis)]
    dot_general x6 -> x10, matrix products: 41.1 us -> 39.7 us  [the longest x3 21.7 us: dot_t(): lax.dot_general(left, right, (((1,), (1,)), ((), ())), preferred_element_...]
  transfers between devices with their start and end apart: 13 -> 15, of which waited for: 13 -> 12; matrix products, arithmetic and copies ran while one was open for 7% -> 12% of each run, Pallas kernels for 0% -> 0%
where the time goes in v1:
time: 457 us; the launch traced here: 455 us
  waiting for transfers between devices  339 us (74%)
  matrix products  39.7 us (9%)
  starting transfers between devices  35 us (8%)
  other arithmetic  17.6 us (4%)
  between operations  13.9 us (3%)
  local copies, waits for them, and re-layouts  10.6 us (2%)
    all_to_all x9, waiting for transfers between devices, exchange(): return lax.all_to_all(blocks, axis, split_axis=0, concat_axis=0, tiled=True)  221 us
    all_gather x1, waiting for transfers between devices, shards(): up_shared = lax.all_gather(shared_up, 'fsdp', axis=0, tiled=True)  42.1 us
    all_gather x1, waiting for transfers between devices, shards(): vit_first = lax.all_gather(vit_fc1, 'fsdp', axis=0, tiled=True)  38.6 us
    all_to_all x9, starting transfers between devices, exchange(): return lax.all_to_all(blocks, axis, split_axis=0, concat_axis=0, tiled=True)  34.8 us
    all_gather x1, waiting for transfers between devices, shards(): vit_second = lax.all_gather(vit_fc2, 'fsdp', axis=0, tiled=True)  34.7 us
    dot_general x3, matrix products, dot_t(): lax.dot_general(left, right, (((1,), (1,)), ((), ())), preferred_element_...  21.7 us
    dot_general x6, matrix products, dot(): return jnp.dot(left, right, preferred_element_type=f32)  13.7 us
  transfers between devices with their start and end apart: 15, of which 12 were waited for; matrix products, arithmetic and copies ran while one was open for 12% of the time, Pallas kernels for 0%

profile of v1, /device:TPU:0, one launch (start us, length us, event | category | flops | bytes accessed | tf_op | source)
XLA Modules:
  0.0 455.2 jit_solution(5039765403945625924)
XLA Ops:
  7.3 38.6 %all-gather.7.cloned.1.call-done = bf16[1152,1076]{1,0:T(8,128)(2,1)} async-done(((bf16[144,1076]{1,0:T(8,128)(2,1)}), bf16[1152,1076]{1,0:T(8,128)(2,1)}) %all-gather.7.cloned.1.call-update) | async-done | bytes 2479120 | tf_op jit(solution)/shard_map/all_gather | solution.py:73
  46.0 34.7 %all-gather.9.cloned.1.call-done = bf16[1152,1076]{1,0:T(8,128)(2,1)} async-done(((bf16[144,1076]{1,0:T(8,128)(2,1)}), bf16[1152,1076]{1,0:T(8,128)(2,1)}) %all-gather.9.cloned.1.call-update) | async-done | bytes 2479120 | tf_op jit(solution)/shard_map/all_gather | solution.py:75
  83.6 11.6 %convolution_convert_fusion = bf16[1024,1152]{1,0:T(8,128)(2,1)} fusion(bf16[1152,1076]{1,0:T(8,128)(2,1)} %all-gather.9.cloned.1.call-done, bf16[1152,1076]{1,0:T(8,128)(2,1)} %all-gather.7.cloned.1.call-done, bf16[1,1024,1152]{2,1,0:T(8,128)(2,1)S(1)} %copy-done.1, f32[1152]{0:T(1024)S(1)} %copy-done.10, f32[1024]{0:T(1024)S(1)} %add_rsqrt_fusion, ...), kind=kOutput, calls=%fused_computation.26 | convolution fusion | flops 5094199296 | bytes 9689600 | tf_op jit(solution)/shard_map/dot_general | solution.py:42
  95.2 4.5 all-to-all-start
  102.4 25.8 %all-to-all-done = bf16[4,256,1152]{2,1,0:T(8,128)(2,1)} async-done(((bf16[4,256,1152]{2,1,0:T(8,128)(2,1)}), bf16[4,256,1152]{2,1,0:T(8,128)(2,1)}, u32[]{:S(2)}, u32[]{:S(2)}) %all-to-all-start) | async-done | bytes 2359328 | tf_op jit(solution)/shard_map/all_to_all | solution.py:34
  138.0 3.6 all-to-all-start.1
  142.2 26.9 %all-to-all-done.1 = bf16[4,64,4608]{2,1,0:T(8,128)(2,1)S(1)} async-done(((bf16[4,64,4608]{2,1,0:T(8,128)(2,1)}), bf16[4,64,4608]{2,1,0:T(8,128)(2,1)S(1)}, u32[]{:S(2)}, u32[]{:S(2)}) %all-to-all-start.1) | async-done | bytes 2359328 | tf_op jit(solution)/shard_map/all_to_all | solution.py:34
  171.7 4.6 %all-to-all-start.3 = ((bf16[4,128,2048]{2,1,0:T(8,128)(2,1)}), bf16[4,128,2048]{2,1,0:T(8,128)(2,1)}, u32[]{:S(2)}, u32[]{:S(2)}) async-start(bf16[4,128,2048]{2,1,0:T(8,128)(2,1)} %broadcast_in_dim.50), calls=%async_computation.3 | async-start | bytes 4194304 | tf_op jit(solution)/shard_map/all_to_all | solution.py:34
  176.4 3.8 convolution_convert_fusion.6
  180.3 20.3 %all-to-all-done.3 = bf16[4,128,2048]{2,1,0:T(8,128)(2,1)} async-done(((bf16[4,128,2048]{2,1,0:T(8,128)(2,1)}), bf16[4,128,2048]{2,1,0:T(8,128)(2,1)}, u32[]{:S(2)}, u32[]{:S(2)}) %all-to-all-start.3) | async-done | bytes 2097184 | tf_op jit(solution)/shard_map/all_to_all | solution.py:34
  201.7 3.5 all-to-all-start.2
  205.8 12.4 %all-to-all-done.2 = bf16[4,256,512]{1,2,0:T(8,128)(2,1)S(1)} async-done(((bf16[4,256,512]{1,2,0:T(8,128)(2,1)}), bf16[4,256,512]{1,2,0:T(8,128)(2,1)S(1)}, u32[]{:S(2)}, u32[]{:S(2)}) %all-to-all-start.2) | async-done | bytes 1048608 | tf_op jit(solution)/shard_map/all_to_all | solution.py:34
  226.4 9.1 %all-to-all-done.4 = bf16[8,64,256]{2,1,0:T(8,128)(2,1)S(1)} async-done(((bf16[8,64,256]{2,1,0:T(8,128)(2,1)}), bf16[8,64,256]{2,1,0:T(8,128)(2,1)S(1)}, u32[]{:S(2)}, u32[]{:S(2)}) %all-to-all-start.4) | async-done | bytes 262176 | tf_op jit(solution)/shard_map/all_to_all | solution.py:34
  238.4 4.4 all-to-all-start.5
  242.9 42.1 %all-gather.15.cloned.1.call-done = bf16[2048,704]{0,1:T(8,128)(2,1)} async-done(((bf16[256,704]{0,1:T(8,128)(2,1)}), bf16[2048,704]{0,1:T(8,128)(2,1)}) %all-gather.15.cloned.1.call-update) | async-done | bytes 2883600 | tf_op jit(solution)/shard_map/all_gather | solution.py:81
  285.1 62.9 %all-to-all-done.5 = bf16[8,64,2816]{2,1,0:T(8,128)(2,1)} async-done(((bf16[8,64,2816]{2,1,0:T(8,128)(2,1)}), bf16[8,64,2816]{2,1,0:T(8,128)(2,1)}, u32[]{:S(2)}, u32[]{:S(2)}) %all-to-all-start.5) | async-done | bytes 2883616 | tf_op jit(solution)/shard_map/all_to_all | solution.py:34
  351.6 3.6 all-to-all-start.6
  355.3 34.9 %all-to-all-done.6 = bf16[8,64,1408]{2,1,0:T(8,128)(2,1)S(1)} async-done(((bf16[8,64,1408]{2,1,0:T(8,128)(2,1)}), bf16[8,64,1408]{2,1,0:T(8,128)(2,1)S(1)}, u32[]{:S(2)}, u32[]{:S(2)}) %all-to-all-start.6) | async-done | bytes 1441824 | tf_op jit(solution)/shard_map/all_to_all | solution.py:34
  394.9 5.5 %fusion.56 = f32[512,704]{0,1:T(8,128)} fusion(bf16[2048,704]{0,1:T(8,128)(2,1)} %all-gather.13.cloned.1.call-done, bf16[512,2048]{1,0:T(8,128)(2,1)} %copy-done.3, f32[2048]{0:T(1024)S(1)} %copy-done.11, f32[512]{0:T(512)S(1)} %add_rsqrt_fusion.1), kind=kOutput, calls=%fused_computation.88 | convolution fusion | flops 1480589312 | bytes 6432768 | tf_op jit(solution)/shard_map/dot_general | solution.py:46
  400.4 4.2 all-to-all-done.7
  404.6 8.7 %fusion.32 = f32[512,2048]{1,0:T(8,128)} fusion(bf16[2048,704]{0,1:T(8,128)(2,1)} %all-gather.17.cloned.1.call-done, bf16[2048,704]{0,1:T(8,128)(2,1)} %all-gather.15.cloned.1.call-done, f32[512,704]{0,1:T(8,128)} %fusion.56, bf16[512,2048]{1,0:T(8,128)(2,1)S(1)} %copy-done.4, f32[2048]{0:T(1024)S(1)} %copy-done.11, f32[512]{0:T(512)S(1)} %add_rsqrt_fusion.1), kind=kOutput, calls=%fused_computation.51 | convolution fusion | flops 2959147008 | bytes 13510656 | tf_op jit(solution)/shard_map/dot_general | solution.py:42
  413.4 4.3 add_convert_fusion
  417.7 3.7 all-to-all-start.8
  421.3 24.7 %all-to-all-done.8 = bf16[4,128,2048]{2,1,0:T(8,128)(2,1)S(1)} async-done(((bf16[4,128,2048]{2,1,0:T(8,128)(2,1)}), bf16[4,128,2048]{2,1,0:T(8,128)(2,1)S(1)}, u32[]{:S(2)}, u32[]{:S(2)}) %all-to-all-start.8) | async-done | bytes 2097184 | tf_op jit(solution)/shard_map/all_to_all | solution.py:34
  (88 shorter events, 42.8 us)
Async XLA Ops:
  6.5 228.9 %copy-start = (bf16[256,1,1408]{2,0,1:T(8,128)(2,1)S(1)}, bf16[256,1,1408]{2,0,1:T(8,128)(2,1)}, u32[]{:S(2)}) copy-start(bf16[256,1,1408]{2,0,1:T(8,128)(2,1)} %param.34) | copy-start | bytes 2162692
  6.5 76.3 %copy-start.1 = (bf16[1,1024,1152]{2,1,0:T(8,128)(2,1)S(1)}, bf16[1,1024,1152]{2,1,0:T(8,128)(2,1)}, u32[]{:S(2)}) copy-start(bf16[1,1024,1152]{2,1,0:T(8,128)(2,1)} %param.18) | copy-start | bytes 7077892
  6.5 39.4 %all-gather.7.cloned.1.call-start = ((), (), s32[]{:S(2)}) async-start(), calls=%async_computation.9 | async-start | bytes 2985984 | tf_op jit(solution)/shard_map/all_gather | solution.py:73
  7.3 73.4 %all-gather.9.cloned.1.call-start = ((), (), s32[]{:S(2)}) async-start(), calls=%async_computation.10 | async-start | bytes 2985984 | tf_op jit(solution)/shard_map/all_gather | solution.py:75
  45.9 95.7 %all-gather.11.cloned.1.call-start = ((), (), s32[]{:S(2)}) async-start(), calls=%async_computation.11 | async-start | bytes 5308416 | tf_op jit(solution)/shard_map/all_gather | solution.py:77
  95.2 32.9 %all-to-all-start = ((bf16[4,256,1152]{2,1,0:T(8,128)(2,1)}), bf16[4,256,1152]{2,1,0:T(8,128)(2,1)}, u32[]{:S(2)}, u32[]{:S(2)}) async-start(bf16[4,256,1152]{2,1,0:T(8,128)(2,1)} %bitcast.78), calls=%async_computation | async-start | bytes 4718592 | tf_op jit(solution)/shard_map/all_to_all | solution.py:34
  138.0 31.1 %all-to-all-start.1 = ((bf16[4,64,4608]{2,1,0:T(8,128)(2,1)}), bf16[4,64,4608]{2,1,0:T(8,128)(2,1)S(1)}, u32[]{:S(2)}, u32[]{:S(2)}) async-start(bf16[4,64,4608]{2,1,0:T(8,128)(2,1)} %broadcast_in_dim.46), calls=%async_computation.1 | async-start | bytes 4718592 | tf_op jit(solution)/shard_map/all_to_all | solution.py:34
  141.6 84.3 %all-gather.13.cloned.1.call-start = ((), (), s32[]{:S(2)}) async-start(), calls=%async_computation.12 | async-start | bytes 3244032 | tf_op jit(solution)/shard_map/all_gather | solution.py:79
  171.7 28.9 %all-to-all-start.3 = ((bf16[4,128,2048]{2,1,0:T(8,128)(2,1)}), bf16[4,128,2048]{2,1,0:T(8,128)(2,1)}, u32[]{:S(2)}, u32[]{:S(2)}) async-start(bf16[4,128,2048]{2,1,0:T(8,128)(2,1)} %broadcast_in_dim.50), calls=%async_computation.3 | async-start | bytes 4194304 | tf_op jit(solution)/shard_map/all_to_all | solution.py:34
  180.1 25.1 %copy-start.5 = (s32[1,512,6]{1,0,2:T(1,128)S(1)}, s32[1,512,6]{1,0,2:T(1,128)}, u32[]{:S(2)}) copy-start(s32[1,512,6]{1,0,2:T(1,128)} %param.22) | copy-start | bytes 36868
  180.2 25.3 %copy-start.12 = (s32[1,4]{1,0:T(1,128)S(1)}, s32[1,4]{1,0:T(1,128)}, u32[]{:S(2)}) copy-start(s32[1,4]{1,0:T(1,128)} %param.19) | copy-start | bytes 52
  180.2 25.4 %copy-start.8 = (s32[1,4]{1,0:T(1,128)S(1)}, s32[1,4]{1,0:T(1,128)}, u32[]{:S(2)}) copy-start(s32[1,4]{1,0:T(1,128)} %param.20) | copy-start | bytes 52
  201.7 16.6 %all-to-all-start.2 = ((bf16[4,256,512]{1,2,0:T(8,128)(2,1)}), bf16[4,256,512]{1,2,0:T(8,128)(2,1)S(1)}, u32[]{:S(2)}, u32[]{:S(2)}) async-start(bf16[4,256,512]{1,2,0:T(8,128)(2,1)} %broadcast_in_dim.48), calls=%async_computation.2 | async-start | bytes 2097152 | tf_op jit(solution)/shard_map/all_to_all | solution.py:34
  221.6 14.4 %copy-start.2 = (bf16[256,1,1408]{2,0,1:T(8,128)(2,1)S(1)}, bf16[256,1,1408]{2,0,1:T(8,128)(2,1)}, u32[]{:S(2)}) copy-start(bf16[256,1,1408]{2,0,1:T(8,128)(2,1)} %param.33) | copy-start | bytes 2162692
  222.4 13.1 %all-to-all-start.4 = ((bf16[8,64,256]{2,1,0:T(8,128)(2,1)}), bf16[8,64,256]{2,1,0:T(8,128)(2,1)S(1)}, u32[]{:S(2)}, u32[]{:S(2)}) async-start(bf16[8,64,256]{2,1,0:T(8,128)(2,1)} %bitcast.77), calls=%async_computation.4 | async-start | bytes 524288 | tf_op jit(solution)/shard_map/all_to_all | solution.py:34
  225.8 59.3 %all-gather.15.cloned.1.call-start = ((), (), s32[]{:S(2)}) async-start(), calls=%async_computation.13 | async-start | bytes 3244032 | tf_op jit(solution)/shard_map/all_gather | solution.py:81
  238.4 109.6 %all-to-all-start.5 = ((bf16[8,64,2816]{2,1,0:T(8,128)(2,1)}), bf16[8,64,2816]{2,1,0:T(8,128)(2,1)}, u32[]{:S(2)}, u32[]{:S(2)}) async-start(bf16[8,64,2816]{2,1,0:T(8,128)(2,1)} %pad_maximum_fusion), calls=%async_computation.5 | async-start | bytes 5767168 | tf_op jit(solution)/shard_map/all_to_all | solution.py:34
  242.8 161.8 %all-gather.17.cloned.1.call-start = ((), (), s32[]{:S(2)}) async-start(), calls=%async_computation.14 | async-start | bytes 3244032 | tf_op jit(solution)/shard_map/all_gather | solution.py:83
  350.4 4.8 %copy-start.7 = (f32[1,512,6]{1,0,2:T(1,128)S(1)}, f32[1,512,6]{1,0,2:T(1,128)}, u32[]{:S(2)}) copy-start(f32[1,512,6]{1,0,2:T(1,128)} %param.23) | copy-start | bytes 36868
  350.4 39.7 %copy-start.9 = (bf16[256,1,1408]{2,0,1:T(8,128)(2,1)S(1)}, bf16[256,1,1408]{2,0,1:T(8,128)(2,1)}, u32[]{:S(2)}) copy-start(bf16[256,1,1408]{2,0,1:T(8,128)(2,1)} %param.35) | copy-start | bytes 2162692
  351.6 38.5 %all-to-all-start.6 = ((bf16[8,64,1408]{2,1,0:T(8,128)(2,1)}), bf16[8,64,1408]{2,1,0:T(8,128)(2,1)S(1)}, u32[]{:S(2)}, u32[]{:S(2)}) async-start(bf16[8,64,1408]{2,1,0:T(8,128)(2,1)} %broadcast_in_dim.51), calls=%async_computation.6 | async-start | bytes 2883584 | tf_op jit(solution)/shard_map/all_to_all | solution.py:34
  391.5 13.1 %all-to-all-start.7 = ((bf16[8,64,256]{2,1,0:T(8,128)(2,1)}), bf16[8,64,256]{2,1,0:T(8,128)(2,1)S(1)}, u32[]{:S(2)}, u32[]{:S(2)}) async-start(bf16[8,64,256]{2,1,0:T(8,128)(2,1)} %bitcast.19), calls=%async_computation.7 | async-start | bytes 524288 | tf_op jit(solution)/shard_map/all_to_all | solution.py:34
  394.9 9.7 %copy-start.4 = (bf16[512,2048]{1,0:T(8,128)(2,1)S(1)}, bf16[512,2048]{1,0:T(8,128)(2,1)}, u32[]{:S(2)}) copy-start(bf16[512,2048]{1,0:T(8,128)(2,1)} %copy-done.3) | copy-start | bytes 6291460
  417.7 28.4 %all-to-all-start.8 = ((bf16[4,128,2048]{2,1,0:T(8,128)(2,1)}), bf16[4,128,2048]{2,1,0:T(8,128)(2,1)S(1)}, u32[]{:S(2)}, u32[]{:S(2)}) async-start(bf16[4,128,2048]{2,1,0:T(8,128)(2,1)} %bitcast.21), calls=%async_computation.8 | async-start | bytes 4194304 | tf_op jit(solution)/shard_map/all_to_all | solution.py:34
  (4 other events, 10.3 us)
Sparse Core Ops, SparseCore 0:
  9.0 36.8 all-gather.6
  47.5 33.1 all-gather.8
  82.4 50.6 all-gather.10
  143.7 36.5 all-gather.12
  227.9 57.0 all-gather.14
  286.5 60.0 all-gather.16

commit v2 on v1

--- a/solution.py
+++ b/solution.py
@@ -30,12 +30,14 @@
     return jnp.sum(jnp.where(inside, placed, 0), axis=1)
 
 
-def exchange(blocks, axis):
-    return lax.all_to_all(blocks, axis, split_axis=0, concat_axis=0, tiled=True)
-
-
-def spread_blocks(block, axis, count):
-    return exchange(jnp.broadcast_to(block[None], (count,) + block.shape), axis)
+def exchange(blocks, axis, groups=None):
+    return lax.all_to_all(
+        blocks, axis, split_axis=0, concat_axis=0, tiled=True, axis_index_groups=groups
+    )
+
+
+def spread_blocks(block, axis, count, groups=None):
+    return exchange(jnp.broadcast_to(block[None], (count,) + block.shape), axis, groups)
 
 
 def dot_t(left, right):
@@ -70,22 +72,22 @@
     me = lax.axis_index("seq")
     n_fsdp = lax.axis_size("fsdp")
 
-    vit_first = lax.all_gather(vit_fc1, "fsdp", axis=0, tiled=True)
-    vit_fc2, vit_first = lax.optimization_barrier((vit_fc2, vit_first))
-    vit_second = lax.all_gather(vit_fc2, "fsdp", axis=0, tiled=True)
-    proj_weight, vit_second = lax.optimization_barrier((proj_weight, vit_second))
-    projector = lax.all_gather(proj_weight, "fsdp", axis=0, tiled=True)
-    shared_gate, projector = lax.optimization_barrier((shared_gate, projector))
-    gate_shared = lax.all_gather(shared_gate, "fsdp", axis=0, tiled=True)
-    shared_up, gate_shared = lax.optimization_barrier((shared_up, gate_shared))
-    up_shared = lax.all_gather(shared_up, "fsdp", axis=0, tiled=True)
-    shared_down, up_shared = lax.optimization_barrier((shared_down, up_shared))
-    down_shared = lax.all_gather(shared_down, "fsdp", axis=0, tiled=True)
+    half = n_fsdp // 2
+    swap = [(i, i ^ 1) for i in range(n_fsdp)]
+    lines = [[2 * i + c for i in range(half)] for c in range(2)]
 
     width = embeds.shape[2]
     tok_dev = embeds.shape[1]
     all_embeds = spread_blocks(embeds[0], "seq", n_seq).reshape(n_seq * tok_dev, width)
     n_tok = n_seq * tok_dev
+
+    vit_both = lax.all_gather(jnp.stack([vit_fc1, vit_fc2]), "fsdp", axis=1, tiled=True)
+    proj_weight, vit_both, all_embeds = lax.optimization_barrier(
+        (proj_weight, vit_both, all_embeds)
+    )
+    vit_first, vit_second = vit_both[0], vit_both[1]
+    projector = lax.all_gather(proj_weight, "fsdp", axis=0, tiled=True)
+    shared = jnp.stack([shared_gate, shared_up, shared_down])
 
     rows = patches.shape[1]
     my_rows = rows // n_seq
@@ -93,6 +95,9 @@
     hidden = jax.nn.gelu(dot(normed, vit_first), approximate=True).astype(bf16)
     product = dot_t(hidden, vit_second).astype(bf16)
     blocks = exchange(product.reshape(n_seq, my_rows, product.shape[1]), "seq")
+    shared, blocks = lax.optimization_barrier((shared, blocks))
+    shared = lax.all_gather(shared, "fsdp", axis=1, tiled=True)
+    gate_shared, up_shared, down_shared = shared[0], shared[1], shared[2]
     mixed = jnp.sum(blocks.astype(f32), axis=0)
     mine = lax.dynamic_slice_in_dim(patches[0], me * my_rows, my_rows, axis=0)
     residual = mine.astype(f32) + mixed
@@ -112,38 +117,62 @@
     merged = jnp.where(is_visual[:, None], placed_visual, all_embeds)
     tokens = rms_norm(merged.astype(f32), moe_gain).astype(bf16)
 
+    shared_hidden = (jax.nn.silu(dot(tokens, gate_shared)) * dot(tokens, up_shared)).astype(bf16)
+    shared_value = dot_t(shared_hidden, down_shared).astype(bf16)
+    terms = exchange(shared_value.reshape(n_seq, tok_dev, width), "seq")
+
     capacity = n_tok // 8
-    hit_mask = route_ids[0] == me
-    chosen = jnp.any(hit_mask, axis=1)
-    weight_sum = jnp.sum(jnp.where(hit_mask, route_weights[0], 0.0), axis=1)
-    before = (token_ids[None, :] < token_ids[:, None]) & chosen[None, :]
-    rank = jnp.sum(before.astype(f32), axis=1).astype(jnp.int32)
+    experts = jnp.arange(n_seq, dtype=jnp.int32)
+    hit_mask = route_ids[0][None] == experts[:, None, None]
+    chosen = jnp.any(hit_mask, axis=2)
+    weight_sum = jnp.sum(jnp.where(hit_mask, route_weights[0][None], 0.0), axis=2)
+    earlier = (token_ids[:, None] < token_ids[None, :]).astype(bf16)
+    rank = dot(chosen.astype(bf16), earlier).astype(jnp.int32)
+    rank = jnp.where(chosen, rank, -1)
     slot_ids = jnp.arange(capacity, dtype=jnp.int32)
-    pick = chosen[None, :] & (rank[None, :] == slot_ids[:, None])
+    my_rank = lax.dynamic_index_in_dim(rank, me, 0, keepdims=False)
+    pick = my_rank[None, :] == slot_ids[:, None]
+
     picked = dot(pick.astype(bf16), tokens).astype(bf16)
     depth = expert_gate.shape[0]
     hid = expert_gate.shape[2]
+    core = lax.axis_index("fsdp") % 2
     picked_cols = exchange(picked.reshape(capacity, n_fsdp, depth).transpose(1, 0, 2), "fsdp")
+    picked_cols = picked_cols.reshape(half, 2, capacity, depth).transpose(1, 0, 2, 3)
     picked_cols = picked_cols.reshape(n_fsdp * capacity, depth)
     gate_up = jnp.concatenate(
         [dot(picked_cols, expert_gate[:, 0, :]), dot(picked_cols, expert_up[:, 0, :])], axis=1
     ).astype(bf16)
-    sums = jnp.sum(exchange(gate_up.reshape(n_fsdp, capacity, 2 * hid), "fsdp").astype(f32), axis=0)
+    gate_up = gate_up.reshape(2, half * capacity, 2 * hid)
+    keep = lax.dynamic_index_in_dim(gate_up, core, 0, keepdims=False)
+    sent = lax.dynamic_index_in_dim(gate_up, 1 - core, 0, keepdims=False)
+    sent = lax.ppermute(sent, "fsdp", swap)
+    gate_up = (keep.astype(f32) + sent.astype(f32)).astype(bf16)
+    gate_up = exchange(gate_up.reshape(half, capacity, 2 * hid), "fsdp", lines)
+    sums = jnp.sum(gate_up.astype(f32), axis=0)
     expert_hidden = (jax.nn.silu(sums[:, :hid]) * sums[:, hid:]).astype(bf16)
-    all_hidden = spread_blocks(expert_hidden, "fsdp", n_fsdp).reshape(n_fsdp * capacity, hid)
+    line_hidden = spread_blocks(expert_hidden, "fsdp", half, lines)
+    other_hidden = lax.ppermute(line_hidden, "fsdp", swap)
+    all_hidden = jnp.stack(
+        [
+            jnp.where(core == 0, line_hidden, other_hidden),
+            jnp.where(core == 0, other_hidden, line_hidden),
+        ]
+    ).reshape(n_fsdp * capacity, hid)
     down_cols = dot_t(all_hidden, expert_down[:, 0, :]).astype(bf16)
+    down_cols = down_cols.reshape(2, half, capacity, depth).transpose(1, 0, 2, 3)
     values = exchange(down_cols.reshape(n_fsdp, capacity, depth), "fsdp")
     values = values.transpose(1, 0, 2).reshape(capacity, width)
-    routed = lax.dot_general(
-        pick.astype(bf16), values, (((0,), (0,)), ((), ())), preferred_element_type=f32
-    )
-
-    shared_hidden = (jax.nn.silu(dot(tokens, gate_shared)) * dot(tokens, up_shared)).astype(bf16)
-    partial_value = (dot_t(shared_hidden, down_shared) + routed * weight_sum[:, None]).astype(bf16)
-    terms = exchange(partial_value.reshape(n_seq, tok_dev, width), "seq")
-    summed = jnp.sum(terms.astype(f32), axis=0)
+
+    all_values = spread_blocks(values, "seq", n_seq)
+    own_rank = lax.dynamic_slice_in_dim(rank, me * tok_dev, tok_dev, axis=1)
+    own_weight = lax.dynamic_slice_in_dim(weight_sum, me * tok_dev, tok_dev, axis=1)
+    total = jnp.sum(terms.astype(f32), axis=0)
+    for e in range(n_seq):
+        back = own_rank[e][:, None] == slot_ids[None, :]
+        total = total + dot(back.astype(bf16), all_values[e]) * own_weight[e][:, None]
     own = lax.dynamic_slice_in_dim(merged, me * tok_dev, tok_dev, axis=0)
-    return (own.astype(f32) + summed).astype(bf16)[None]
+    return (own.astype(f32) + total).astype(bf16)[None]
 
 
 def solution(mesh):

time: 457 us -> 351 us (0.77)
  waiting for transfers between devices: 339 us -> 152 us
  blocking collectives: 0 us -> 88.7 us
  starting transfers between devices: 35 us -> 27.8 us
    all_to_all x9 -> x7, waiting for transfers between devices: 221 us -> 118 us  [exchange(): lax.all_to_all(blocks, axis, split_axis=0, concat_axis=0, tiled=True, axi...]
    all_to_all x0 -> x3, blocking collectives: none -> 88.7 us  [exchange(): lax.all_to_all(blocks, axis, split_axis=0, concat_axis=0, tiled=True, axi...]
    all_gather x5 -> x2, waiting for transfers between devices: 116 us -> 28.7 us  [the longest x1 28.6 us: shards(): lax.all_gather(jnp.stack([vit_fc1, vit_fc2]), 'fsdp', axis=1, tiled=True)]
    all_to_all x9 -> x7, starting transfers between devices: 34.8 us -> 27.5 us  [exchange(): lax.all_to_all(blocks, axis, split_axis=0, concat_axis=0, tiled=True, axi...]
    dot_general x6 -> x11, matrix products: 13.7 us -> 19.3 us  [dot(): return jnp.dot(left, right, preferred_element_type=f32)]
    ppermute x0 -> x2, waiting for transfers between devices: none -> 5.54 us  [the longest x1 3.36 us: shards(): sent = lax.ppermute(sent, 'fsdp', swap)]
  transfers between devices with their start and end apart: 15 -> 12, of which waited for: 12 -> 9; matrix products, arithmetic and copies ran while one was open for 12% -> 16% of each run, Pallas kernels for 0% -> 0%
where the time goes in v2:
time: 351 us; the launch traced here: 349 us
  waiting for transfers between devices  152 us (43%)
  blocking collectives  88.7 us (25%)
  matrix products  39.6 us (11%)
  starting transfers between devices  27.8 us (8%)
  other arithmetic  17.5 us (5%)
  between operations  13.7 us (4%)
  local copies, waits for them, and re-layouts  10 us (3%)
    all_to_all x7, waiting for transfers between devices, exchange(): lax.all_to_all(blocks, axis, split_axis=0, concat_axis=0, tiled=True, axi...  118 us
    all_to_all x3, blocking collectives, exchange(): lax.all_to_all(blocks, axis, split_axis=0, concat_axis=0, tiled=True, axi...  88.7 us
    all_gather x1, waiting for transfers between devices, shards(): lax.all_gather(jnp.stack([vit_fc1, vit_fc2]), 'fsdp', axis=1, tiled=True)  28.6 us
    all_to_all x7, starting transfers between devices, exchange(): lax.all_to_all(blocks, axis, split_axis=0, concat_axis=0, tiled=True, axi...  27.5 us
    dot_general x3, matrix products, dot_t(): lax.dot_general(left, right, (((1,), (1,)), ((), ())), preferred_element_...  20.3 us
    dot_general x11, matrix products, dot(): return jnp.dot(left, right, preferred_element_type=f32)  19.3 us
  transfers between devices with their start and end apart: 12, of which 9 were waited for; matrix products, arithmetic and copies ran while one was open for 16% of the time, Pallas kernels for 0%

profile of v2, /device:TPU:0, one launch (start us, length us, event | category | flops | bytes accessed | tf_op | source)
XLA Modules:
  0.0 349.4 jit_solution(16928309893945531297)
XLA Ops:
  9.0 30.6 %all_to_all.50 = bf16[4,128,2048]{2,1,0:T(8,128)(2,1)} all-to-all(bf16[4,128,2048]{2,1,0:T(8,128)(2,1)S(1)} %broadcast_in_dim.66), channel_id=1, replica_groups=mesh['seq'=4,'fsdp'=8] {'seq'}, dimensions={0} | all-to-all | bytes 4194304 | tf_op jit(solution)/shard_map/all_to_all | solution.py:34
  39.6 28.6 %all-gather.4.cloned.1.call-done = bf16[2,1152,1076]{2,1,0:T(8,128)(2,1)} async-done(((bf16[2,144,1076]{2,1,0:T(8,128)(2,1)}), bf16[2,1152,1076]{2,1,0:T(8,128)(2,1)}) %all-gather.4.cloned.1.call-update) | async-done | bytes 4958224 | tf_op jit(solution)/shard_map/all_gather | solution.py:84
  69.5 11.6 %convolution_convert_fusion = bf16[1024,1152]{1,0:T(8,128)(2,1)} fusion(bf16[2,1152,1076]{2,1,0:T(8,128)(2,1)} %all-gather.4.cloned.1.call-done, bf16[1,1024,1152]{2,1,0:T(8,128)(2,1)S(1)} %copy-done.2, f32[1152]{0:T(1024)S(1)} %copy-done.17, f32[1024]{0:T(1024)S(1)} %add_rsqrt_fusion, f32[1024]{0:T(1024)S(1)} %broadcast_multiply_fusion), kind=kOutput, calls=%fused_computation.25 | convolution fusion | flops 5094199296 | bytes 9689600 | tf_op jit(solution)/shard_map/dot_general | solution.py:44
  81.1 4.5 %all-to-all-start.1 = ((bf16[4,256,1152]{2,1,0:T(8,128)(2,1)}), bf16[4,256,1152]{2,1,0:T(8,128)(2,1)}, u32[]{:S(2)}, u32[]{:S(2)}) async-start(bf16[4,256,1152]{2,1,0:T(8,128)(2,1)} %bitcast.154), calls=%async_computation.1 | async-start | bytes 4718592 | tf_op jit(solution)/shard_map/all_to_all | solution.py:34
  89.6 24.5 %all-to-all-done.1 = bf16[4,256,1152]{2,1,0:T(8,128)(2,1)} async-done(((bf16[4,256,1152]{2,1,0:T(8,128)(2,1)}), bf16[4,256,1152]{2,1,0:T(8,128)(2,1)}, u32[]{:S(2)}, u32[]{:S(2)}) %all-to-all-start.1) | async-done | bytes 2359328 | tf_op jit(solution)/shard_map/all_to_all | solution.py:34
  123.8 3.9 %all-to-all-start.2 = ((bf16[4,64,4608]{2,1,0:T(8,128)(2,1)}), bf16[4,64,4608]{2,1,0:T(8,128)(2,1)S(1)}, u32[]{:S(2)}, u32[]{:S(2)}) async-start(bf16[4,64,4608]{2,1,0:T(8,128)(2,1)} %broadcast_in_dim.67), calls=%async_computation.2 | async-start | bytes 4718592 | tf_op jit(solution)/shard_map/all_to_all | solution.py:34
  127.8 27.5 %all-to-all-done.2 = bf16[4,64,4608]{2,1,0:T(8,128)(2,1)S(1)} async-done(((bf16[4,64,4608]{2,1,0:T(8,128)(2,1)}), bf16[4,64,4608]{2,1,0:T(8,128)(2,1)S(1)}, u32[]{:S(2)}, u32[]{:S(2)}) %all-to-all-start.2) | async-done | bytes 2359328 | tf_op jit(solution)/shard_map/all_to_all | solution.py:34
  155.2 3.7 %convolution_convert_fusion.7 = bf16[256,512]{1,0:T(8,128)(2,1)S(1)} fusion(bf16[256,4608]{1,0:T(8,128)(2,1)S(1)} %bitcast.155, bf16[4608,512]{1,0:T(8,128)(2,1)} %all-gather.6.cloned.1.call-done), kind=kOutput, calls=%fused_computation.72 | convolution fusion | flops 1208090624 | bytes 7340032 | tf_op jit(solution)/shard_map/dot_general | solution.py:48
  160.2 4.3 %all-to-all-start.3 = ((bf16[4,256,512]{1,2,0:T(8,128)(2,1)}), bf16[4,256,512]{1,2,0:T(8,128)(2,1)}, u32[]{:S(2)}, u32[]{:S(2)}) async-start(bf16[4,256,512]{1,2,0:T(8,128)(2,1)} %broadcast_in_dim.68), calls=%async_computation.3 | async-start | bytes 2097152 | tf_op jit(solution)/shard_map/all_to_all | solution.py:34
  165.1 12.7 %all-to-all-done.3 = bf16[4,256,512]{1,2,0:T(8,128)(2,1)} async-done(((bf16[4,256,512]{1,2,0:T(8,128)(2,1)}), bf16[4,256,512]{1,2,0:T(8,128)(2,1)}, u32[]{:S(2)}, u32[]{:S(2)}) %all-to-all-start.3) | async-done | bytes 1048608 | tf_op jit(solution)/shard_map/all_to_all | solution.py:34
  177.7 2.2 fusion.14
  181.5 3.4 all-to-all-start.5
  184.9 15.4 %all-to-all-done.5 = bf16[8,64,256]{2,1,0:T(8,128)(2,1)S(1)} async-done(((bf16[8,64,256]{2,1,0:T(8,128)(2,1)}), bf16[8,64,256]{2,1,0:T(8,128)(2,1)S(1)}, u32[]{:S(2)}, u32[]{:S(2)}) %all-to-all-start.5) | async-done | bytes 262176 | tf_op jit(solution)/shard_map/all_to_all | solution.py:34
  204.0 3.4 collective-permute-done
  209.2 37.2 %all_to_all.51 = bf16[4,64,2816]{2,1,0:T(8,128)(2,1)S(1)} all-to-all(bf16[4,64,2816]{2,1,0:T(8,128)(2,1)S(1)} %bitcast.151), channel_id=1, replica_groups={{0,2,4,6},{1,3,5,7},{8,10,12,14},{9,11,13,15},{16,18,20,22},{17,19,21,2..., dimensions={0} | all-to-all | bytes 2883584 | tf_op jit(solution)/shard_map/all_to_all | solution.py:34
  246.8 20.9 %all_to_all.52 = bf16[4,64,1408]{2,1,0:T(8,128)(2,1)S(1)} all-to-all(bf16[4,64,1408]{2,1,0:T(8,128)(2,1)S(1)} %broadcast_in_dim.70), channel_id=1, replica_groups={{0,2,4,6},{1,3,5,7},{8,10,12,14},{9,11,13,15},{16,18,20,22},{17,19,21,2..., dimensions={0} | all-to-all | bytes 1441792 | tf_op jit(solution)/shard_map/all_to_all | solution.py:34
  271.6 3.4 all-to-all-start.8
  275.1 4.7 %fusion.18 = f32[512,704]{0,1:T(8,128)} fusion(bf16[3,2048,704]{1,2,0:T(8,128)(2,1)} %all-gather.8.cloned.1.call-done, bf16[512,2048]{1,0:T(8,128)(2,1)S(1)} %copy-done.11, f32[2048]{0:T(1024)S(1)} %copy-done.18, f32[512]{0:T(512)S(1)} %add_rsqrt_fusion.1), kind=kOutput, calls=%fused_computation.38 | convolution fusion | flops 1480589312 | bytes 6432768 | tf_op jit(solution)/shard_map/dot_general | solution.py:48
  279.8 8.0 %convolution_convert_fusion.4 = bf16[512,2048]{1,0:T(8,128)(2,1)} fusion(bf16[3,2048,704]{1,2,0:T(8,128)(2,1)} %all-gather.8.cloned.1.call-done, f32[512,704]{0,1:T(8,128)} %fusion.18, bf16[512,2048]{1,0:T(8,128)(2,1)S(1)} %copy-done.11, f32[2048]{0:T(1024)S(1)} %copy-done.18, f32[512]{0:T(512)S(1)} %add_rsqrt_fusion.1), kind=kOutput, calls=%fused_computation.33 | convolution fusion | flops 2960195584 | bytes 11413504 | tf_op jit(solution)/shard_map/dot_general | solution.py:44
  287.8 3.7 %all-to-all-start.4 = ((bf16[4,128,2048]{2,1,0:T(8,128)(2,1)}), bf16[4,128,2048]{2,1,0:T(8,128)(2,1)S(1)}, u32[]{:S(2)}, u32[]{:S(2)}) async-start(bf16[4,128,2048]{2,1,0:T(8,128)(2,1)} %bitcast.157), calls=%async_computation.4 | async-start | bytes 4194304 | tf_op jit(solution)/shard_map/all_to_all | solution.py:34
  291.6 25.6 %all-to-all-done.4 = bf16[4,128,2048]{2,1,0:T(8,128)(2,1)S(1)} async-done(((bf16[4,128,2048]{2,1,0:T(8,128)(2,1)}), bf16[4,128,2048]{2,1,0:T(8,128)(2,1)S(1)}, u32[]{:S(2)}, u32[]{:S(2)}) %all-to-all-start.4) | async-done | bytes 2097184 | tf_op jit(solution)/shard_map/all_to_all | solution.py:34
  318.3 4.2 %all-to-all-start.9 = ((bf16[4,64,2048]{2,1,0:T(8,128)(2,1)}), bf16[4,64,2048]{2,1,0:T(8,128)(2,1)}, u32[]{:S(2)}, u32[]{:S(2)}) async-start(bf16[4,64,2048]{2,1,0:T(8,128)(2,1)} %broadcast_in_dim.72), calls=%async_computation.9 | async-start | bytes 2097152 | tf_op jit(solution)/shard_map/all_to_all | solution.py:34
  324.0 12.2 %all-to-all-done.9 = bf16[4,64,2048]{2,1,0:T(8,128)(2,1)} async-done(((bf16[4,64,2048]{2,1,0:T(8,128)(2,1)}), bf16[4,64,2048]{2,1,0:T(8,128)(2,1)}, u32[]{:S(2)}, u32[]{:S(2)}) %all-to-all-start.9) | async-done | bytes 1048608 | tf_op jit(solution)/shard_map/all_to_all | solution.py:34
  340.6 2.3 fusion.39
  (112 shorter events, 37.1 us)
Async XLA Ops:
  6.5 193.8 %copy-start = (bf16[256,1,1408]{2,0,1:T(8,128)(2,1)S(1)}, bf16[256,1,1408]{2,0,1:T(8,128)(2,1)}, u32[]{:S(2)}) copy-start(bf16[256,1,1408]{2,0,1:T(8,128)(2,1)} %param.34) | copy-start | bytes 2162692
  6.5 61.7 %all-gather.4.cloned.1.call-start = ((), (), s32[]{:S(2)}) async-start(), calls=%async_computation.10 | async-start | bytes 5971968 | tf_op jit(solution)/shard_map/all_gather | solution.py:84
  8.7 146.5 %all-gather.6.cloned.1.call-start = ((), (), s32[]{:S(2)}) async-start(), calls=%async_computation.11 | async-start | bytes 5308416 | tf_op jit(solution)/shard_map/all_gather | solution.py:89
  9.0 59.3 %copy-start.2 = (bf16[1,1024,1152]{2,1,0:T(8,128)(2,1)S(1)}, bf16[1,1024,1152]{2,1,0:T(8,128)(2,1)}, u32[]{:S(2)}) copy-start(bf16[1,1024,1152]{2,1,0:T(8,128)(2,1)} %param.18) | copy-start | bytes 7077892
  81.1 32.9 %all-to-all-start.1 = ((bf16[4,256,1152]{2,1,0:T(8,128)(2,1)}), bf16[4,256,1152]{2,1,0:T(8,128)(2,1)}, u32[]{:S(2)}, u32[]{:S(2)}) async-start(bf16[4,256,1152]{2,1,0:T(8,128)(2,1)} %bitcast.154), calls=%async_computation.1 | async-start | bytes 4718592 | tf_op jit(solution)/shard_map/all_to_all | solution.py:34
  85.6 2.7 copy-start.7
  85.6 189.4 %all-gather.8.cloned.1.call-start = ((), (), s32[]{:S(2)}) async-start(), calls=%async_computation.12 | async-start | bytes 9732096 | tf_op jit(solution)/shard_map/all_gather | solution.py:99
  117.4 3.3 copy-start.12
  123.8 4.0 %copy-start.13 = (s32[1,512,6]{1,0,2:T(1,128)S(1)}, s32[1,512,6]{1,0,2:T(1,128)}, u32[]{:S(2)}) copy-start(s32[1,512,6]{1,0,2:T(1,128)} %param.22) | copy-start | bytes 36868
  123.8 31.5 %all-to-all-start.2 = ((bf16[4,64,4608]{2,1,0:T(8,128)(2,1)}), bf16[4,64,4608]{2,1,0:T(8,128)(2,1)S(1)}, u32[]{:S(2)}, u32[]{:S(2)}) async-start(bf16[4,64,4608]{2,1,0:T(8,128)(2,1)} %broadcast_in_dim.67), calls=%async_computation.2 | async-start | bytes 4718592 | tf_op jit(solution)/shard_map/all_to_all | solution.py:34
  159.0 5.7 %copy-start.19 = (s32[1,4]{1,0:T(1,128)S(1)}, s32[1,4]{1,0:T(1,128)}, u32[]{:S(2)}) copy-start(s32[1,4]{1,0:T(1,128)} %param.19) | copy-start | bytes 52
  159.0 5.8 %copy-start.15 = (s32[1,4]{1,0:T(1,128)S(1)}, s32[1,4]{1,0:T(1,128)}, u32[]{:S(2)}) copy-start(s32[1,4]{1,0:T(1,128)} %param.20) | copy-start | bytes 52
  159.0 18.7 %copy-start.4 = (bf16[4,128,2048]{2,1,0:T(8,128)(2,1)S(1)}, bf16[4,128,2048]{2,1,0:T(8,128)(2,1)}, u32[]{:S(2)}) copy-start(bf16[4,128,2048]{2,1,0:T(8,128)(2,1)} %all_to_all.50) | copy-start | bytes 6291460
  160.2 17.5 %all-to-all-start.3 = ((bf16[4,256,512]{1,2,0:T(8,128)(2,1)}), bf16[4,256,512]{1,2,0:T(8,128)(2,1)}, u32[]{:S(2)}, u32[]{:S(2)}) async-start(bf16[4,256,512]{1,2,0:T(8,128)(2,1)} %broadcast_in_dim.68), calls=%async_computation.3 | async-start | bytes 2097152 | tf_op jit(solution)/shard_map/all_to_all | solution.py:34
  180.7 20.1 %copy-start.5 = (bf16[256,1,1408]{2,0,1:T(8,128)(2,1)S(1)}, bf16[256,1,1408]{2,0,1:T(8,128)(2,1)}, u32[]{:S(2)}) copy-start(bf16[256,1,1408]{2,0,1:T(8,128)(2,1)} %param.33) | copy-start | bytes 2162692
  181.5 18.8 %all-to-all-start.5 = ((bf16[8,64,256]{2,1,0:T(8,128)(2,1)}), bf16[8,64,256]{2,1,0:T(8,128)(2,1)S(1)}, u32[]{:S(2)}, u32[]{:S(2)}) async-start(bf16[8,64,256]{2,1,0:T(8,128)(2,1)} %bitcast.148), calls=%async_computation.5 | async-start | bytes 524288 | tf_op jit(solution)/shard_map/all_to_all | solution.py:34
  203.8 3.6 %collective-permute-start = (bf16[256,2816]{1,0:T(8,128)(2,1)}, bf16[256,2816]{1,0:T(8,128)(2,1)}, u32[]{:S(2)}, u32[]{:S(2)}) collective-permute-start(bf16[256,2816]{1,0:T(8,128)(2,1)} %fusion.42), channel_id=1, source_target_pairs={{0,1},{1,0},{2,3},{3,2},{4,5},{5,4},{6,7},{7,6},{8,9},{9,8},{10,11... | collective-permute-start | bytes 4325384 | tf_op jit(solution)/shard_map/ppermute | solution.py:149
  267.8 2.2 collective-permute-start.1
  270.2 4.8 %copy-start.11 = (bf16[512,2048]{1,0:T(8,128)(2,1)S(1)}, bf16[512,2048]{1,0:T(8,128)(2,1)}, u32[]{:S(2)}) copy-start(bf16[512,2048]{1,0:T(8,128)(2,1)} %copy-done.10) | copy-start | bytes 6291460
  271.6 16.2 %all-to-all-start.8 = ((bf16[8,64,256]{2,1,0:T(8,128)(2,1)}), bf16[8,64,256]{2,1,0:T(8,128)(2,1)S(1)}, u32[]{:S(2)}, u32[]{:S(2)}) async-start(bf16[8,64,256]{2,1,0:T(8,128)(2,1)} %bitcast.44), calls=%async_computation.8 | async-start | bytes 524288 | tf_op jit(solution)/shard_map/all_to_all | solution.py:34
  287.8 3.8 %copy-start.14 = (f32[1,512,6]{1,0,2:T(1,128)S(1)}, f32[1,512,6]{1,0,2:T(1,128)}, u32[]{:S(2)}) copy-start(f32[1,512,6]{1,0,2:T(1,128)} %param.23) | copy-start | bytes 36868
  287.8 29.4 %all-to-all-start.4 = ((bf16[4,128,2048]{2,1,0:T(8,128)(2,1)}), bf16[4,128,2048]{2,1,0:T(8,128)(2,1)S(1)}, u32[]{:S(2)}, u32[]{:S(2)}) async-start(bf16[4,128,2048]{2,1,0:T(8,128)(2,1)} %bitcast.157), calls=%async_computation.4 | async-start | bytes 4194304 | tf_op jit(solution)/shard_map/all_to_all | solution.py:34
  318.3 17.9 %all-to-all-start.9 = ((bf16[4,64,2048]{2,1,0:T(8,128)(2,1)}), bf16[4,64,2048]{2,1,0:T(8,128)(2,1)}, u32[]{:S(2)}, u32[]{:S(2)}) async-start(bf16[4,64,2048]{2,1,0:T(8,128)(2,1)} %broadcast_in_dim.72), calls=%async_computation.9 | async-start | bytes 2097152 | tf_op jit(solution)/shard_map/all_to_all | solution.py:34
  339.2 3.7 %copy-start.1 = (bf16[256,1,1408]{2,0,1:T(8,128)(2,1)S(1)}, bf16[256,1,1408]{2,0,1:T(8,128)(2,1)}, u32[]{:S(2)}) copy-start(bf16[256,1,1408]{2,0,1:T(8,128)(2,1)} %param.34) | copy-start | bytes 2162692
  (8 other events, 13.9 us)
Sparse Core Ops, SparseCore 0:
  9.0 59.2 all-gather.3
  69.9 50.5 all-gather.5
  122.0 89.0 all-gather.7

commit v3 on v2

--- a/solution.py
+++ b/solution.py
@@ -1,3 +1,5 @@
+import functools
+
 import jax
 import jax.numpy as jnp
 from jax import lax
@@ -30,14 +32,12 @@
     return jnp.sum(jnp.where(inside, placed, 0), axis=1)
 
 
-def exchange(blocks, axis, groups=None):
-    return lax.all_to_all(
-        blocks, axis, split_axis=0, concat_axis=0, tiled=True, axis_index_groups=groups
-    )
-
-
-def spread_blocks(block, axis, count, groups=None):
-    return exchange(jnp.broadcast_to(block[None], (count,) + block.shape), axis, groups)
+def exchange(blocks, axis):
+    return lax.all_to_all(blocks, axis, split_axis=0, concat_axis=0, tiled=True)
+
+
+def spread_blocks(block, axis, count):
+    return exchange(jnp.broadcast_to(block[None], (count,) + block.shape), axis)
 
 
 def dot_t(left, right):
@@ -74,7 +74,7 @@
 
     half = n_fsdp // 2
     swap = [(i, i ^ 1) for i in range(n_fsdp)]
-    lines = [[2 * i + c for i in range(half)] for c in range(2)]
+    shifts = [[(i, (i + 2 * k) % n_fsdp) for i in range(n_fsdp)] for k in range(half)]
 
     width = embeds.shape[2]
     tok_dev = embeds.shape[1]
@@ -119,7 +119,6 @@
 
     shared_hidden = (jax.nn.silu(dot(tokens, gate_shared)) * dot(tokens, up_shared)).astype(bf16)
     shared_value = dot_t(shared_hidden, down_shared).astype(bf16)
-    terms = exchange(shared_value.reshape(n_seq, tok_dev, width), "seq")
 
     capacity = n_tok // 8
     experts = jnp.arange(n_seq, dtype=jnp.int32)
@@ -148,19 +147,26 @@
     sent = lax.dynamic_index_in_dim(gate_up, 1 - core, 0, keepdims=False)
     sent = lax.ppermute(sent, "fsdp", swap)
     gate_up = (keep.astype(f32) + sent.astype(f32)).astype(bf16)
-    gate_up = exchange(gate_up.reshape(half, capacity, 2 * hid), "fsdp", lines)
-    sums = jnp.sum(gate_up.astype(f32), axis=0)
+    gate_up = gate_up.reshape(half, capacity, 2 * hid)
+    here = lax.axis_index("fsdp") // 2
+    gate_up = jnp.concatenate([gate_up, gate_up], axis=0)
+    gate_up = lax.dynamic_slice_in_dim(gate_up, here, half, axis=0)
+    arrived = [gate_up[0]] + [lax.ppermute(gate_up[k], "fsdp", shifts[k]) for k in range(1, half)]
+    shared_value, arrived = lax.optimization_barrier((shared_value, arrived))
+    terms = exchange(shared_value.reshape(n_seq, tok_dev, width), "seq")
+    sums = functools.reduce(jnp.add, [part.astype(f32) for part in arrived])
     expert_hidden = (jax.nn.silu(sums[:, :hid]) * sums[:, hid:]).astype(bf16)
-    line_hidden = spread_blocks(expert_hidden, "fsdp", half, lines)
-    other_hidden = lax.ppermute(line_hidden, "fsdp", swap)
-    all_hidden = jnp.stack(
-        [
-            jnp.where(core == 0, line_hidden, other_hidden),
-            jnp.where(core == 0, other_hidden, line_hidden),
-        ]
-    ).reshape(n_fsdp * capacity, hid)
+    line_hidden = [expert_hidden]
+    line_hidden += [lax.ppermute(expert_hidden, "fsdp", shifts[k]) for k in range(1, half)]
+    other_hidden = [lax.ppermute(part, "fsdp", swap) for part in line_hidden]
+    terms, other_hidden = lax.optimization_barrier((terms, other_hidden))
+    all_hidden = jnp.concatenate(line_hidden[::-1] + other_hidden[::-1], axis=0)
     down_cols = dot_t(all_hidden, expert_down[:, 0, :]).astype(bf16)
-    down_cols = down_cols.reshape(2, half, capacity, depth).transpose(1, 0, 2, 3)
+    down_cols = down_cols.reshape(2, half, capacity, depth)
+    down_cols = jnp.concatenate([down_cols, down_cols], axis=1)
+    down_cols = lax.dynamic_slice_in_dim(down_cols, half - 1 - here, half, axis=1)
+    down_cols = jnp.concatenate([down_cols, down_cols], axis=0)
+    down_cols = lax.dynamic_slice_in_dim(down_cols, core, 2, axis=0).transpose(1, 0, 2, 3)
     values = exchange(down_cols.reshape(n_fsdp, capacity, depth), "fsdp")
     values = values.transpose(1, 0, 2).reshape(capacity, width)
 

time: 351 us -> 329 us (0.937)
  blocking collectives: 88.7 us -> 30.6 us
  starting transfers between devices: 27.8 us -> 42.5 us
  local copies, waits for them, and re-layouts: 10 us -> 19 us
  waiting for transfers between devices: 152 us -> 159 us
    all_to_all x3 -> x1, blocking collectives: 88.7 us -> 30.6 us  [exchange(): return lax.all_to_all(blocks, axis, split_axis=0, concat_axis=0, tiled=True)]
    ppermute x1 -> x10, waiting for transfers between devices: 2.19 us -> 25.3 us  [the longest x3 15.3 us: shards(): lax.ppermute(expert_hidden, 'fsdp', shifts[k])]
    all_to_all x7, waiting for transfers between devices: 118 us -> 101 us  [exchange(): return lax.all_to_all(blocks, axis, split_axis=0, concat_axis=0, tiled=True)]
    ppermute x1 -> x10, starting transfers between devices: 0.01 us -> 12.7 us  [the longest x3 8.84 us: shards(): lax.ppermute(expert_hidden, 'fsdp', shifts[k])]
    unnamed x42 -> x61, local copies, waits for them, and re-layouts: 1.2 us -> 8.69 us
  transfers between devices with their start and end apart: 12 -> 21, of which waited for: 9 -> 12; matrix products, arithmetic and copies ran while one was open for 16% -> 18% of each run, Pallas kernels for 0% -> 0%
where the time goes in v3:
time: 329 us; the launch traced here: 328 us
  waiting for transfers between devices  159 us (48%)
  starting transfers between devices  42.5 us (13%)
  matrix products  42.4 us (13%)
  blocking collectives  30.6 us (9%)
  other arithmetic  20.3 us (6%)
  local copies, waits for them, and re-layouts  19 us (6%)
  between operations  13.7 us (4%)
    all_to_all x7, waiting for transfers between devices, exchange(): return lax.all_to_all(blocks, axis, split_axis=0, concat_axis=0, tiled=True)  101 us
    all_to_all x1, blocking collectives, exchange(): return lax.all_to_all(blocks, axis, split_axis=0, concat_axis=0, tiled=True)  30.6 us
    all_to_all x7, starting transfers between devices, exchange(): return lax.all_to_all(blocks, axis, split_axis=0, concat_axis=0, tiled=True)  29.7 us
    all_gather x1, waiting for transfers between devices, shards(): lax.all_gather(jnp.stack([vit_fc1, vit_fc2]), 'fsdp', axis=1, tiled=True)  28.7 us
    dot_general x3, matrix products, dot_t(): lax.dot_general(left, right, (((1,), (1,)), ((), ())), preferred_element_...  22.4 us
    dot_general x11, matrix products, dot(): return jnp.dot(left, right, preferred_element_type=f32)  20 us
    ppermute x3, waiting for transfers between devices, shards(): lax.ppermute(expert_hidden, 'fsdp', shifts[k])  15.3 us
    ppermute x3, waiting for transfers between devices, shards(): lax.ppermute(gate_up[k], 'fsdp', shifts[k])  10.1 us
  transfers between devices with their start and end apart: 21, of which 12 were waited for; matrix products, arithmetic and copies ran while one was open for 18% of the time, Pallas kernels for 0%

profile of v3, /device:TPU:0, one launch (start us, length us, event | category | flops | bytes accessed | tf_op | source)
XLA Modules:
  0.0 327.6 jit_solution(8180136411621777990)
XLA Ops:
  9.0 30.6 %all_to_all.40 = bf16[4,128,2048]{2,1,0:T(8,128)(2,1)} all-to-all(bf16[4,128,2048]{2,1,0:T(8,128)(2,1)S(1)} %broadcast_in_dim.64), channel_id=1, replica_groups=mesh['seq'=4,'fsdp'=8] {'seq'}, dimensions={0} | all-to-all | bytes 4194304 | tf_op jit(solution)/shard_map/all_to_all | solution.py:36
  39.6 28.7 %all-gather.4.cloned.1.call-done = bf16[2,1152,1076]{2,1,0:T(8,128)(2,1)} async-done(((bf16[2,144,1076]{2,1,0:T(8,128)(2,1)}), bf16[2,1152,1076]{2,1,0:T(8,128)(2,1)}) %all-gather.4.cloned.1.call-update) | async-done | bytes 4958224 | tf_op jit(solution)/shard_map/all_gather | solution.py:84
  69.5 11.6 %convolution_convert_fusion = bf16[1024,1152]{1,0:T(8,128)(2,1)} fusion(bf16[2,1152,1076]{2,1,0:T(8,128)(2,1)} %all-gather.4.cloned.1.call-done, bf16[1,1024,1152]{2,1,0:T(8,128)(2,1)S(1)} %copy-done.2, f32[1152]{0:T(1024)S(1)} %copy-done.22, f32[1024]{0:T(1024)S(1)} %add_rsqrt_fusion, f32[1024]{0:T(1024)S(1)} %broadcast_multiply_fusion), kind=kOutput, calls=%fused_computation.25 | convolution fusion | flops 5094199296 | bytes 9689600 | tf_op jit(solution)/shard_map/dot_general | solution.py:44
  81.1 4.6 %all-to-all-start.1 = ((bf16[4,256,1152]{2,1,0:T(8,128)(2,1)}), bf16[4,256,1152]{2,1,0:T(8,128)(2,1)}, u32[]{:S(2)}, u32[]{:S(2)}) async-start(bf16[4,256,1152]{2,1,0:T(8,128)(2,1)} %bitcast.158), calls=%async_computation.1 | async-start | bytes 4718592 | tf_op jit(solution)/shard_map/all_to_all | solution.py:36
  88.0 26.1 %all-to-all-done.1 = bf16[4,256,1152]{2,1,0:T(8,128)(2,1)} async-done(((bf16[4,256,1152]{2,1,0:T(8,128)(2,1)}), bf16[4,256,1152]{2,1,0:T(8,128)(2,1)}, u32[]{:S(2)}, u32[]{:S(2)}) %all-to-all-start.1) | async-done | bytes 2359328 | tf_op jit(solution)/shard_map/all_to_all | solution.py:36
  126.5 4.0 %all-to-all-start.2 = ((bf16[4,64,4608]{2,1,0:T(8,128)(2,1)}), bf16[4,64,4608]{2,1,0:T(8,128)(2,1)S(1)}, u32[]{:S(2)}, u32[]{:S(2)}) async-start(bf16[4,64,4608]{2,1,0:T(8,128)(2,1)} %broadcast_in_dim.65), calls=%async_computation.2 | async-start | bytes 4718592 | tf_op jit(solution)/shard_map/all_to_all | solution.py:36
  130.5 27.5 %all-to-all-done.2 = bf16[4,64,4608]{2,1,0:T(8,128)(2,1)S(1)} async-done(((bf16[4,64,4608]{2,1,0:T(8,128)(2,1)}), bf16[4,64,4608]{2,1,0:T(8,128)(2,1)S(1)}, u32[]{:S(2)}, u32[]{:S(2)}) %all-to-all-start.2) | async-done | bytes 2359328 | tf_op jit(solution)/shard_map/all_to_all | solution.py:36
  158.0 3.8 %convolution_convert_fusion.7 = bf16[256,512]{1,0:T(8,128)(2,1)S(1)} fusion(bf16[256,4608]{1,0:T(8,128)(2,1)S(1)} %bitcast.157, bf16[4608,512]{1,0:T(8,128)(2,1)} %all-gather.6.cloned.1.call-done), kind=kOutput, calls=%fused_computation.73 | convolution fusion | flops 1208090624 | bytes 7340032 | tf_op jit(solution)/shard_map/dot_general | solution.py:48
  163.0 4.2 %all-to-all-start.3 = ((bf16[4,256,512]{1,2,0:T(8,128)(2,1)}), bf16[4,256,512]{1,2,0:T(8,128)(2,1)}, u32[]{:S(2)}, u32[]{:S(2)}) async-start(bf16[4,256,512]{1,2,0:T(8,128)(2,1)} %broadcast_in_dim.66), calls=%async_computation.3 | async-start | bytes 2097152 | tf_op jit(solution)/shard_map/all_to_all | solution.py:36
  167.9 12.8 %all-to-all-done.3 = bf16[4,256,512]{1,2,0:T(8,128)(2,1)} async-done(((bf16[4,256,512]{1,2,0:T(8,128)(2,1)}), bf16[4,256,512]{1,2,0:T(8,128)(2,1)}, u32[]{:S(2)}, u32[]{:S(2)}) %all-to-all-start.3) | async-done | bytes 1048608 | tf_op jit(solution)/shard_map/all_to_all | solution.py:36
  184.4 3.4 %all-to-all-start.4 = ((bf16[8,64,256]{2,1,0:T(8,128)(2,1)}), bf16[8,64,256]{2,1,0:T(8,128)(2,1)S(1)}, u32[]{:S(2)}, u32[]{:S(2)}) async-start(bf16[8,64,256]{2,1,0:T(8,128)(2,1)} %bitcast.151), calls=%async_computation.4 | async-start | bytes 524288 | tf_op jit(solution)/shard_map/all_to_all | solution.py:36
  187.9 13.8 %all-to-all-done.4 = bf16[8,64,256]{2,1,0:T(8,128)(2,1)S(1)} async-done(((bf16[8,64,256]{2,1,0:T(8,128)(2,1)}), bf16[8,64,256]{2,1,0:T(8,128)(2,1)S(1)}, u32[]{:S(2)}, u32[]{:S(2)}) %all-to-all-start.4) | async-done | bytes 262176 | tf_op jit(solution)/shard_map/all_to_all | solution.py:36
  204.5 3.6 %collective-permute-done = bf16[256,2816]{1,0:T(8,128)(2,1)} collective-permute-done((bf16[256,2816]{1,0:T(8,128)(2,1)}, bf16[256,2816]{1,0:T(8,128)(2,1)}, u32[]{:S(2)}, u32[]{:S(2)}) %collective-permute-start) | collective-permute-done | bytes 1441824 | tf_op jit(solution)/shard_map/ppermute | solution.py:148
  214.5 5.3 %fusion.18 = f32[512,704]{0,1:T(8,128)} fusion(bf16[3,2048,704]{1,2,0:T(8,128)(2,1)} %all-gather.8.cloned.1.call-done, bf16[512,2048]{1,0:T(8,128)(2,1)} %copy-done.13, f32[2048]{0:T(1024)S(1)} %copy-done.24, f32[512]{0:T(512)S(1)} %copy-done.20), kind=kOutput, calls=%fused_computation.38 | convolution fusion | flops 1480589312 | bytes 6432768 | tf_op jit(solution)/shard_map/dot_general | solution.py:48
  219.8 8.6 %convolution_convert_fusion.4 = bf16[512,2048]{1,0:T(8,128)(2,1)} fusion(bf16[3,2048,704]{1,2,0:T(8,128)(2,1)} %all-gather.8.cloned.1.call-done, f32[512,704]{0,1:T(8,128)} %fusion.18, bf16[512,2048]{1,0:T(8,128)(2,1)} %copy-done.13, f32[2048]{0:T(1024)S(1)} %copy-done.24, f32[512]{0:T(512)S(1)} %copy-done.20), kind=kOutput, calls=%fused_computation.33 | convolution fusion | flops 2960195584 | bytes 11413504 | tf_op jit(solution)/shard_map/dot_general | solution.py:44
  228.4 10.1 %collective-permute-done.2 = bf16[64,2816]{1,0:T(8,128)(2,1)S(1)} collective-permute-done((bf16[64,2816]{1,0:T(8,128)(2,1)S(1)}, bf16[64,2816]{1,0:T(8,128)(2,1)S(1)}, u32[]{:S(2)}, u32[]{:S(2)}) %collective-permute-start.2) | collective-permute-done | bytes 360480 | tf_op jit(solution)/shard_map/ppermute | solution.py:154
  239.4 3.6 %all-to-all-start.5 = ((bf16[4,128,2048]{2,1,0:T(8,128)(2,1)}), bf16[4,128,2048]{2,1,0:T(8,128)(2,1)S(1)}, u32[]{:S(2)}, u32[]{:S(2)}) async-start(bf16[4,128,2048]{2,1,0:T(8,128)(2,1)} %bitcast.160), calls=%async_computation.5 | async-start | bytes 4194304 | tf_op jit(solution)/shard_map/all_to_all | solution.py:36
  244.3 6.9 %collective-permute-start.9 = (bf16[64,1408]{1,0:T(8,128)(2,1)S(1)}, bf16[64,1408]{1,0:T(8,128)(2,1)S(1)}, u32[]{:S(2)}, u32[]{:S(2)}) collective-permute-start(bf16[64,1408]{1,0:T(8,128)(2,1)S(1)} %fusion.58), channel_id=1, source_target_pairs={{0,6},{1,7},{2,0},{3,1},{4,2},{5,3},{6,4},{7,5},{8,14},{9,15},{10,... | collective-permute-start | bytes 540680 | tf_op jit(solution)/shard_map/ppermute | solution.py:160
  253.2 6.1 %collective-permute-done.9 = bf16[64,1408]{1,0:T(8,128)(2,1)S(1)} collective-permute-done((bf16[64,1408]{1,0:T(8,128)(2,1)S(1)}, bf16[64,1408]{1,0:T(8,128)(2,1)S(1)}, u32[]{:S(2)}, u32[]{:S(2)}) %collective-permute-start.9) | collective-permute-done | bytes 180256 | tf_op jit(solution)/shard_map/ppermute | solution.py:160
  260.7 7.8 %collective-permute-done.7 = bf16[64,1408]{1,0:T(8,128)(2,1)S(1)} collective-permute-done((bf16[64,1408]{1,0:T(8,128)(2,1)S(1)}, bf16[64,1408]{1,0:T(8,128)(2,1)S(1)}, u32[]{:S(2)}, u32[]{:S(2)}) %collective-permute-start.7) | collective-permute-done | bytes 180256 | tf_op jit(solution)/shard_map/ppermute | solution.py:160
  280.1 5.6 %all-to-all-start.6 = ((bf16[8,64,256]{2,1,0:T(8,128)(2,1)}), bf16[8,64,256]{2,1,0:T(8,128)(2,1)S(1)}, u32[]{:S(2)}, u32[]{:S(2)}) async-start(bf16[8,64,256]{2,1,0:T(8,128)(2,1)} %bitcast.45), calls=%async_computation.6 | async-start | bytes 524288 | tf_op jit(solution)/shard_map/all_to_all | solution.py:36
  285.7 9.7 %all-to-all-done.6 = bf16[8,64,256]{2,1,0:T(8,128)(2,1)S(1)} async-done(((bf16[8,64,256]{2,1,0:T(8,128)(2,1)}), bf16[8,64,256]{2,1,0:T(8,128)(2,1)S(1)}, u32[]{:S(2)}, u32[]{:S(2)}) %all-to-all-start.6) | async-done | bytes 262176 | tf_op jit(solution)/shard_map/all_to_all | solution.py:36
  296.6 4.2 %all-to-all-start.7 = ((bf16[4,64,2048]{2,1,0:T(8,128)(2,1)}), bf16[4,64,2048]{2,1,0:T(8,128)(2,1)}, u32[]{:S(2)}, u32[]{:S(2)}) async-start(bf16[4,64,2048]{2,1,0:T(8,128)(2,1)} %broadcast_in_dim.112), calls=%async_computation.7 | async-start | bytes 2097152 | tf_op jit(solution)/shard_map/all_to_all | solution.py:36
  302.9 11.6 %all-to-all-done.7 = bf16[4,64,2048]{2,1,0:T(8,128)(2,1)} async-done(((bf16[4,64,2048]{2,1,0:T(8,128)(2,1)}), bf16[4,64,2048]{2,1,0:T(8,128)(2,1)}, u32[]{:S(2)}, u32[]{:S(2)}) %all-to-all-start.7) | async-done | bytes 1048608 | tf_op jit(solution)/shard_map/all_to_all | solution.py:36
  (149 shorter events, 59.7 us)
Async XLA Ops:
  6.5 195.2 %copy-start = (bf16[256,1,1408]{2,0,1:T(8,128)(2,1)S(1)}, bf16[256,1,1408]{2,0,1:T(8,128)(2,1)}, u32[]{:S(2)}) copy-start(bf16[256,1,1408]{2,0,1:T(8,128)(2,1)} %param.34) | copy-start | bytes 2162692
  6.5 61.7 %all-gather.4.cloned.1.call-start = ((), (), s32[]{:S(2)}) async-start(), calls=%async_computation.8 | async-start | bytes 5971968 | tf_op jit(solution)/shard_map/all_gather | solution.py:84
  8.7 149.3 %all-gather.6.cloned.1.call-start = ((), (), s32[]{:S(2)}) async-start(), calls=%async_computation.9 | async-start | bytes 5308416 | tf_op jit(solution)/shard_map/all_gather | solution.py:89
  9.0 59.3 %copy-start.2 = (bf16[1,1024,1152]{2,1,0:T(8,128)(2,1)S(1)}, bf16[1,1024,1152]{2,1,0:T(8,128)(2,1)}, u32[]{:S(2)}) copy-start(bf16[1,1024,1152]{2,1,0:T(8,128)(2,1)} %param.18) | copy-start | bytes 7077892
  81.1 33.1 %all-to-all-start.1 = ((bf16[4,256,1152]{2,1,0:T(8,128)(2,1)}), bf16[4,256,1152]{2,1,0:T(8,128)(2,1)}, u32[]{:S(2)}, u32[]{:S(2)}) async-start(bf16[4,256,1152]{2,1,0:T(8,128)(2,1)} %bitcast.158), calls=%async_computation.1 | async-start | bytes 4718592 | tf_op jit(solution)/shard_map/all_to_all | solution.py:36
  85.7 128.7 %all-gather.8.cloned.1.call-start = ((), (), s32[]{:S(2)}) async-start(), calls=%async_computation.10 | async-start | bytes 9732096 | tf_op jit(solution)/shard_map/all_gather | solution.py:99
  126.5 31.5 %all-to-all-start.2 = ((bf16[4,64,4608]{2,1,0:T(8,128)(2,1)}), bf16[4,64,4608]{2,1,0:T(8,128)(2,1)S(1)}, u32[]{:S(2)}, u32[]{:S(2)}) async-start(bf16[4,64,4608]{2,1,0:T(8,128)(2,1)} %broadcast_in_dim.65), calls=%async_computation.2 | async-start | bytes 4718592 | tf_op jit(solution)/shard_map/all_to_all | solution.py:36
  161.8 18.9 %copy-start.4 = (bf16[4,128,2048]{2,1,0:T(8,128)(2,1)S(1)}, bf16[4,128,2048]{2,1,0:T(8,128)(2,1)}, u32[]{:S(2)}) copy-start(bf16[4,128,2048]{2,1,0:T(8,128)(2,1)} %all_to_all.40) | copy-start | bytes 6291460
  163.0 17.6 %all-to-all-start.3 = ((bf16[4,256,512]{1,2,0:T(8,128)(2,1)}), bf16[4,256,512]{1,2,0:T(8,128)(2,1)}, u32[]{:S(2)}, u32[]{:S(2)}) async-start(bf16[4,256,512]{1,2,0:T(8,128)(2,1)} %broadcast_in_dim.66), calls=%async_computation.3 | async-start | bytes 2097152 | tf_op jit(solution)/shard_map/all_to_all | solution.py:36
  184.4 17.2 %all-to-all-start.4 = ((bf16[8,64,256]{2,1,0:T(8,128)(2,1)}), bf16[8,64,256]{2,1,0:T(8,128)(2,1)S(1)}, u32[]{:S(2)}, u32[]{:S(2)}) async-start(bf16[8,64,256]{2,1,0:T(8,128)(2,1)} %bitcast.151), calls=%async_computation.4 | async-start | bytes 524288 | tf_op jit(solution)/shard_map/all_to_all | solution.py:36
  204.5 3.6 %collective-permute-start = (bf16[256,2816]{1,0:T(8,128)(2,1)}, bf16[256,2816]{1,0:T(8,128)(2,1)}, u32[]{:S(2)}, u32[]{:S(2)}) collective-permute-start(bf16[256,2816]{1,0:T(8,128)(2,1)} %fusion.43), channel_id=1, source_target_pairs={{0,1},{1,0},{2,3},{3,2},{4,5},{5,4},{6,7},{7,6},{8,9},{9,8},{10,11... | collective-permute-start | bytes 4325384 | tf_op jit(solution)/shard_map/ppermute | solution.py:148
  210.6 17.9 %collective-permute-start.1 = (bf16[64,2816]{1,0:T(8,128)(2,1)S(1)}, bf16[64,2816]{1,0:T(8,128)(2,1)S(1)}, u32[]{:S(2)}, u32[]{:S(2)}) collective-permute-start(bf16[64,2816]{1,0:T(8,128)(2,1)S(1)} %get-tuple-element.37), channel_id=1, source_target_pairs={{0,2},{1,3},{2,4},{3,5},{4,6},{5,7},{6,0},{7,1},{8,10},{9,11},{10,... | collective-permute-start | bytes 1081352 | tf_op jit(solution)/shard_map/ppermute | solution.py:154
  211.1 27.4 %collective-permute-start.2 = (bf16[64,2816]{1,0:T(8,128)(2,1)S(1)}, bf16[64,2816]{1,0:T(8,128)(2,1)S(1)}, u32[]{:S(2)}, u32[]{:S(2)}) collective-permute-start(bf16[64,2816]{1,0:T(8,128)(2,1)S(1)} %get-tuple-element.36), channel_id=1, source_target_pairs={{0,4},{1,5},{2,6},{3,7},{4,0},{5,1},{6,2},{7,3},{8,12},{9,13},{10,... | collective-permute-start | bytes 1081352 | tf_op jit(solution)/shard_map/ppermute | solution.py:154
  211.4 27.1 %collective-permute-start.3 = (bf16[64,2816]{1,0:T(8,128)(2,1)S(1)}, bf16[64,2816]{1,0:T(8,128)(2,1)S(1)}, u32[]{:S(2)}, u32[]{:S(2)}) collective-permute-start(bf16[64,2816]{1,0:T(8,128)(2,1)S(1)} %get-tuple-element.35), channel_id=1, source_target_pairs={{0,6},{1,7},{2,0},{3,1},{4,2},{5,3},{6,4},{7,5},{8,14},{9,15},{10,... | collective-permute-start | bytes 1081352 | tf_op jit(solution)/shard_map/ppermute | solution.py:154
  239.4 31.2 %all-to-all-start.5 = ((bf16[4,128,2048]{2,1,0:T(8,128)(2,1)}), bf16[4,128,2048]{2,1,0:T(8,128)(2,1)S(1)}, u32[]{:S(2)}, u32[]{:S(2)}) async-start(bf16[4,128,2048]{2,1,0:T(8,128)(2,1)} %bitcast.160), calls=%async_computation.5 | async-start | bytes 4194304 | tf_op jit(solution)/shard_map/all_to_all | solution.py:36
  244.3 15.0 %collective-permute-start.9 = (bf16[64,1408]{1,0:T(8,128)(2,1)S(1)}, bf16[64,1408]{1,0:T(8,128)(2,1)S(1)}, u32[]{:S(2)}, u32[]{:S(2)}) collective-permute-start(bf16[64,1408]{1,0:T(8,128)(2,1)S(1)} %fusion.58), channel_id=1, source_target_pairs={{0,6},{1,7},{2,0},{3,1},{4,2},{5,3},{6,4},{7,5},{8,14},{9,15},{10,... | collective-permute-start | bytes 540680 | tf_op jit(solution)/shard_map/ppermute | solution.py:160
  251.2 9.4 %collective-permute-start.5 = (bf16[64,1408]{1,0:T(8,128)(2,1)S(1)}, bf16[64,1408]{1,0:T(8,128)(2,1)S(1)}, u32[]{:S(2)}, u32[]{:S(2)}) collective-permute-start(bf16[64,1408]{1,0:T(8,128)(2,1)S(1)} %fusion.58), channel_id=1, source_target_pairs={{0,2},{1,3},{2,4},{3,5},{4,6},{5,7},{6,0},{7,1},{8,10},{9,11},{10,... | collective-permute-start | bytes 540680 | tf_op jit(solution)/shard_map/ppermute | solution.py:160
  252.0 16.5 %collective-permute-start.7 = (bf16[64,1408]{1,0:T(8,128)(2,1)S(1)}, bf16[64,1408]{1,0:T(8,128)(2,1)S(1)}, u32[]{:S(2)}, u32[]{:S(2)}) collective-permute-start(bf16[64,1408]{1,0:T(8,128)(2,1)S(1)} %fusion.58), channel_id=1, source_target_pairs={{0,4},{1,5},{2,6},{3,7},{4,0},{5,1},{6,2},{7,3},{8,12},{9,13},{10,... | collective-permute-start | bytes 540680 | tf_op jit(solution)/shard_map/ppermute | solution.py:160
  253.2 15.5 %collective-permute-start.4 = (bf16[64,1408]{1,0:T(8,128)(2,1)S(1)}, bf16[64,1408]{1,0:T(8,128)(2,1)S(1)}, u32[]{:S(2)}, u32[]{:S(2)}) collective-permute-start(bf16[64,1408]{1,0:T(8,128)(2,1)S(1)} %fusion.58), channel_id=1, source_target_pairs={{0,1},{1,0},{2,3},{3,2},{4,5},{5,4},{6,7},{7,6},{8,9},{9,8},{10,11... | collective-permute-start | bytes 540680 | tf_op jit(solution)/shard_map/ppermute | solution.py:161
  259.3 9.4 %collective-permute-start.10 = (bf16[64,1408]{1,0:T(8,128)(2,1)S(1)}, bf16[64,1408]{1,0:T(8,128)(2,1)S(1)}, u32[]{:S(2)}, u32[]{:S(2)}) collective-permute-start(bf16[64,1408]{1,0:T(8,128)(2,1)S(1)} %collective-permute-done.9), channel_id=1, source_target_pairs={{0,1},{1,0},{2,3},{3,2},{4,5},{5,4},{6,7},{7,6},{8,9},{9,8},{10,11... | collective-permute-start | bytes 540680 | tf_op jit(solution)/shard_map/ppermute | solution.py:161
  260.7 8.1 %collective-permute-start.6 = (bf16[64,1408]{1,0:T(8,128)(2,1)S(1)}, bf16[64,1408]{1,0:T(8,128)(2,1)S(1)}, u32[]{:S(2)}, u32[]{:S(2)}) collective-permute-start(bf16[64,1408]{1,0:T(8,128)(2,1)S(1)} %collective-permute-done.5), channel_id=1, source_target_pairs={{0,1},{1,0},{2,3},{3,2},{4,5},{5,4},{6,7},{7,6},{8,9},{9,8},{10,11... | collective-permute-start | bytes 540680 | tf_op jit(solution)/shard_map/ppermute | solution.py:161
  268.5 2.1 collective-permute-start.8
  280.1 15.3 %all-to-all-start.6 = ((bf16[8,64,256]{2,1,0:T(8,128)(2,1)}), bf16[8,64,256]{2,1,0:T(8,128)(2,1)S(1)}, u32[]{:S(2)}, u32[]{:S(2)}) async-start(bf16[8,64,256]{2,1,0:T(8,128)(2,1)} %bitcast.45), calls=%async_computation.6 | async-start | bytes 524288 | tf_op jit(solution)/shard_map/all_to_all | solution.py:36
  296.6 17.9 %all-to-all-start.7 = ((bf16[4,64,2048]{2,1,0:T(8,128)(2,1)}), bf16[4,64,2048]{2,1,0:T(8,128)(2,1)}, u32[]{:S(2)}, u32[]{:S(2)}) async-start(bf16[4,64,2048]{2,1,0:T(8,128)(2,1)} %broadcast_in_dim.112), calls=%async_computation.7 | async-start | bytes 2097152 | tf_op jit(solution)/shard_map/all_to_all | solution.py:36
  (23 other events, 94.0 us)
Sparse Core Ops, SparseCore 0:
  9.0 59.2 all-gather.3
  69.9 50.5 all-gather.5
  122.0 89.0 all-gather.7

commit v4 on v3

--- a/solution.py
+++ b/solution.py
@@ -160,8 +160,9 @@
     line_hidden += [lax.ppermute(expert_hidden, "fsdp", shifts[k]) for k in range(1, half)]
     other_hidden = [lax.ppermute(part, "fsdp", swap) for part in line_hidden]
     terms, other_hidden = lax.optimization_barrier((terms, other_hidden))
-    all_hidden = jnp.concatenate(line_hidden[::-1] + other_hidden[::-1], axis=0)
-    down_cols = dot_t(all_hidden, expert_down[:, 0, :]).astype(bf16)
+    weights = expert_down[:, 0, :]
+    parts = [dot_t(part, weights).astype(bf16) for part in line_hidden[::-1] + other_hidden[::-1]]
+    down_cols = jnp.stack(parts)
     down_cols = down_cols.reshape(2, half, capacity, depth)
     down_cols = jnp.concatenate([down_cols, down_cols], axis=1)
     down_cols = lax.dynamic_slice_in_dim(down_cols, half - 1 - here, half, axis=1)
@@ -169,14 +170,16 @@
     down_cols = lax.dynamic_slice_in_dim(down_cols, core, 2, axis=0).transpose(1, 0, 2, 3)
     values = exchange(down_cols.reshape(n_fsdp, capacity, depth), "fsdp")
     values = values.transpose(1, 0, 2).reshape(capacity, width)
+    my_weight = lax.dynamic_index_in_dim(weight_sum, me, 0, keepdims=False)
+    slot_weight = jnp.sum(jnp.where(pick, my_weight[None, :], 0.0), axis=1)
+    values = (values.astype(f32) * slot_weight[:, None]).astype(bf16)
 
     all_values = spread_blocks(values, "seq", n_seq)
     own_rank = lax.dynamic_slice_in_dim(rank, me * tok_dev, tok_dev, axis=1)
-    own_weight = lax.dynamic_slice_in_dim(weight_sum, me * tok_dev, tok_dev, axis=1)
+    back = own_rank.T[:, :, None] == slot_ids[None, None, :]
+    back = back.astype(bf16).reshape(tok_dev, n_seq * capacity)
     total = jnp.sum(terms.astype(f32), axis=0)
-    for e in range(n_seq):
-        back = own_rank[e][:, None] == slot_ids[None, :]
-        total = total + dot(back.astype(bf16), all_values[e]) * own_weight[e][:, None]
+    total = total + dot(back, all_values.reshape(n_seq * capacity, width))
     own = lax.dynamic_slice_in_dim(merged, me * tok_dev, tok_dev, axis=0)
     return (own.astype(f32) + total).astype(bf16)[None]
 

time: 329 us -> 324 us (0.985)
  local copies, waits for them, and re-layouts: 19 us -> 12.9 us
    dot_general x3 -> x10, matrix products: 22.4 us -> 27.7 us  [dot_t(): lax.dot_general(left, right, (((1,), (1,)), ((), ())), preferred_element_...]
    unnamed x61 -> x57, local copies, waits for them, and re-layouts: 8.69 us -> 4.13 us
    dot_general x11 -> x8, matrix products: 20 us -> 17.3 us  [dot(): return jnp.dot(left, right, preferred_element_type=f32)]
  transfers between devices with their start and end apart: 21 -> 21, of which waited for: 12 -> 12; matrix products, arithmetic and copies ran while one was open for 18% -> 20% of each run, Pallas kernels for 0% -> 0%
where the time goes in v4:
time: 324 us; the launch traced here: 323 us
  waiting for transfers between devices  159 us (49%)
  matrix products  45 us (14%)
  starting transfers between devices  40.7 us (13%)
  blocking collectives  30.6 us (9%)
  other arithmetic  20.4 us (6%)
  between operations  13.8 us (4%)
  local copies, waits for them, and re-layouts  12.9 us (4%)
    all_to_all x7, waiting for transfers between devices, exchange(): return lax.all_to_all(blocks, axis, split_axis=0, concat_axis=0, tiled=True)  101 us
    all_to_all x1, blocking collectives, exchange(): return lax.all_to_all(blocks, axis, split_axis=0, concat_axis=0, tiled=True)  30.6 us
    all_gather x1, waiting for transfers between devices, shards(): lax.all_gather(jnp.stack([vit_fc1, vit_fc2]), 'fsdp', axis=1, tiled=True)  28.7 us
    dot_general x10, matrix products, dot_t(): lax.dot_general(left, right, (((1,), (1,)), ((), ())), preferred_element_...  27.7 us
    all_to_all x7, starting transfers between devices, exchange(): return lax.all_to_all(blocks, axis, split_axis=0, concat_axis=0, tiled=True)  27.5 us
    dot_general x8, matrix products, dot(): return jnp.dot(left, right, preferred_element_type=f32)  17.3 us
    ppermute x3, waiting for transfers between devices, shards(): lax.ppermute(expert_hidden, 'fsdp', shifts[k])  15.7 us
    ppermute x3, waiting for transfers between devices, shards(): lax.ppermute(gate_up[k], 'fsdp', shifts[k])  9.98 us
  transfers between devices with their start and end apart: 21, of which 12 were waited for; matrix products, arithmetic and copies ran while one was open for 20% of the time, Pallas kernels for 0%

profile of v4, /device:TPU:0, one launch (start us, length us, event | category | flops | bytes accessed | tf_op | source)
XLA Modules:
  0.0 322.7 jit_solution(9889850252866189449)
XLA Ops:
  9.0 30.6 %all_to_all.40 = bf16[4,128,2048]{2,1,0:T(8,128)(2,1)} all-to-all(bf16[4,128,2048]{2,1,0:T(8,128)(2,1)S(1)} %broadcast_in_dim.76), channel_id=1, replica_groups=mesh['seq'=4,'fsdp'=8] {'seq'}, dimensions={0} | all-to-all | bytes 4194304 | tf_op jit(solution)/shard_map/all_to_all | solution.py:36
  39.6 28.7 %all-gather.4.cloned.1.call-done = bf16[2,1152,1076]{2,1,0:T(8,128)(2,1)} async-done(((bf16[2,144,1076]{2,1,0:T(8,128)(2,1)}), bf16[2,1152,1076]{2,1,0:T(8,128)(2,1)}) %all-gather.4.cloned.1.call-update) | async-done | bytes 4958224 | tf_op jit(solution)/shard_map/all_gather | solution.py:84
  69.5 11.6 %convolution_convert_fusion = bf16[1024,1152]{1,0:T(8,128)(2,1)} fusion(bf16[2,1152,1076]{2,1,0:T(8,128)(2,1)} %all-gather.4.cloned.1.call-done, bf16[1,1024,1152]{2,1,0:T(8,128)(2,1)S(1)} %copy-done.1, f32[1152]{0:T(1024)S(1)} %copy-done.23, f32[1024]{0:T(1024)S(1)} %add_rsqrt_fusion, f32[1024]{0:T(1024)S(1)} %broadcast_multiply_fusion), kind=kOutput, calls=%fused_computation.25 | convolution fusion | flops 5094199296 | bytes 9689600 | tf_op jit(solution)/shard_map/dot_general | solution.py:44
  81.1 4.6 %all-to-all-start.1 = ((bf16[4,256,1152]{2,1,0:T(8,128)(2,1)}), bf16[4,256,1152]{2,1,0:T(8,128)(2,1)}, u32[]{:S(2)}, u32[]{:S(2)}) async-start(bf16[4,256,1152]{2,1,0:T(8,128)(2,1)} %bitcast.198), calls=%async_computation.1 | async-start | bytes 4718592 | tf_op jit(solution)/shard_map/all_to_all | solution.py:36
  88.0 26.1 %all-to-all-done.1 = bf16[4,256,1152]{2,1,0:T(8,128)(2,1)} async-done(((bf16[4,256,1152]{2,1,0:T(8,128)(2,1)}), bf16[4,256,1152]{2,1,0:T(8,128)(2,1)}, u32[]{:S(2)}, u32[]{:S(2)}) %all-to-all-start.1) | async-done | bytes 2359328 | tf_op jit(solution)/shard_map/all_to_all | solution.py:36
  126.5 4.0 %all-to-all-start.2 = ((bf16[4,64,4608]{2,1,0:T(8,128)(2,1)}), bf16[4,64,4608]{2,1,0:T(8,128)(2,1)S(1)}, u32[]{:S(2)}, u32[]{:S(2)}) async-start(bf16[4,64,4608]{2,1,0:T(8,128)(2,1)} %broadcast_in_dim.77), calls=%async_computation.2 | async-start | bytes 4718592 | tf_op jit(solution)/shard_map/all_to_all | solution.py:36
  130.5 27.5 %all-to-all-done.2 = bf16[4,64,4608]{2,1,0:T(8,128)(2,1)S(1)} async-done(((bf16[4,64,4608]{2,1,0:T(8,128)(2,1)}), bf16[4,64,4608]{2,1,0:T(8,128)(2,1)S(1)}, u32[]{:S(2)}, u32[]{:S(2)}) %all-to-all-start.2) | async-done | bytes 2359328 | tf_op jit(solution)/shard_map/all_to_all | solution.py:36
  158.0 3.8 %convolution_convert_fusion.6 = bf16[256,512]{1,0:T(8,128)(2,1)S(1)} fusion(bf16[256,4608]{1,0:T(8,128)(2,1)S(1)} %bitcast.197, bf16[4608,512]{1,0:T(8,128)(2,1)} %all-gather.6.cloned.1.call-done), kind=kOutput, calls=%fused_computation.66 | convolution fusion | flops 1208090624 | bytes 7340032 | tf_op jit(solution)/shard_map/dot_general | solution.py:48
  163.0 4.2 %all-to-all-start.3 = ((bf16[4,256,512]{1,2,0:T(8,128)(2,1)}), bf16[4,256,512]{1,2,0:T(8,128)(2,1)}, u32[]{:S(2)}, u32[]{:S(2)}) async-start(bf16[4,256,512]{1,2,0:T(8,128)(2,1)} %broadcast_in_dim.122), calls=%async_computation.3 | async-start | bytes 2097152 | tf_op jit(solution)/shard_map/all_to_all | solution.py:36
  167.9 12.8 %all-to-all-done.3 = bf16[4,256,512]{1,2,0:T(8,128)(2,1)} async-done(((bf16[4,256,512]{1,2,0:T(8,128)(2,1)}), bf16[4,256,512]{1,2,0:T(8,128)(2,1)}, u32[]{:S(2)}, u32[]{:S(2)}) %all-to-all-start.3) | async-done | bytes 1048608 | tf_op jit(solution)/shard_map/all_to_all | solution.py:36
  184.5 3.4 %all-to-all-start.4 = ((bf16[8,64,256]{2,1,0:T(8,128)(2,1)}), bf16[8,64,256]{2,1,0:T(8,128)(2,1)S(1)}, u32[]{:S(2)}, u32[]{:S(2)}) async-start(bf16[8,64,256]{2,1,0:T(8,128)(2,1)} %bitcast.191), calls=%async_computation.4 | async-start | bytes 524288 | tf_op jit(solution)/shard_map/all_to_all | solution.py:36
  187.9 13.8 %all-to-all-done.4 = bf16[8,64,256]{2,1,0:T(8,128)(2,1)S(1)} async-done(((bf16[8,64,256]{2,1,0:T(8,128)(2,1)}), bf16[8,64,256]{2,1,0:T(8,128)(2,1)S(1)}, u32[]{:S(2)}, u32[]{:S(2)}) %all-to-all-start.4) | async-done | bytes 262176 | tf_op jit(solution)/shard_map/all_to_all | solution.py:36
  206.3 3.6 %collective-permute-done = bf16[256,2816]{1,0:T(8,128)(2,1)} collective-permute-done((bf16[256,2816]{1,0:T(8,128)(2,1)}, bf16[256,2816]{1,0:T(8,128)(2,1)}, u32[]{:S(2)}, u32[]{:S(2)}) %collective-permute-start) | collective-permute-done | bytes 1441824 | tf_op jit(solution)/shard_map/ppermute | solution.py:148
  216.3 5.3 %fusion.18 = f32[512,704]{0,1:T(8,128)} fusion(bf16[3,2048,704]{1,2,0:T(8,128)(2,1)} %all-gather.8.cloned.1.call-done, bf16[512,2048]{1,0:T(8,128)(2,1)} %copy-done.13, f32[2048]{0:T(1024)S(1)} %copy-done.25, f32[512]{0:T(512)S(1)} %copy-done.21), kind=kOutput, calls=%fused_computation.38 | convolution fusion | flops 1480589312 | bytes 6432768 | tf_op jit(solution)/shard_map/dot_general | solution.py:48
  221.7 8.7 %convolution_convert_fusion.4 = bf16[512,2048]{1,0:T(8,128)(2,1)} fusion(bf16[3,2048,704]{1,2,0:T(8,128)(2,1)} %all-gather.8.cloned.1.call-done, f32[512,704]{0,1:T(8,128)} %fusion.18, bf16[512,2048]{1,0:T(8,128)(2,1)} %copy-done.13, f32[2048]{0:T(1024)S(1)} %copy-done.25, f32[512]{0:T(512)S(1)} %copy-done.21), kind=kOutput, calls=%fused_computation.33 | convolution fusion | flops 2960195584 | bytes 11413504 | tf_op jit(solution)/shard_map/dot_general | solution.py:44
  230.3 10.0 %collective-permute-done.2 = bf16[64,2816]{1,0:T(8,128)(2,1)S(1)} collective-permute-done((bf16[64,2816]{1,0:T(8,128)(2,1)S(1)}, bf16[64,2816]{1,0:T(8,128)(2,1)S(1)}, u32[]{:S(2)}, u32[]{:S(2)}) %collective-permute-start.2) | collective-permute-done | bytes 360480 | tf_op jit(solution)/shard_map/ppermute | solution.py:154
  241.1 3.6 %all-to-all-start.5 = ((bf16[4,128,2048]{2,1,0:T(8,128)(2,1)}), bf16[4,128,2048]{2,1,0:T(8,128)(2,1)S(1)}, u32[]{:S(2)}, u32[]{:S(2)}) async-start(bf16[4,128,2048]{2,1,0:T(8,128)(2,1)} %bitcast.200), calls=%async_computation.5 | async-start | bytes 4194304 | tf_op jit(solution)/shard_map/all_to_all | solution.py:36
  246.1 7.2 %collective-permute-start.9 = (bf16[64,1408]{1,0:T(8,128)(2,1)S(1)}, bf16[64,1408]{1,0:T(8,128)(2,1)S(1)}, u32[]{:S(2)}, u32[]{:S(2)}) collective-permute-start(bf16[64,1408]{1,0:T(8,128)(2,1)S(1)} %fusion.78), channel_id=1, source_target_pairs={{0,6},{1,7},{2,0},{3,1},{4,2},{5,3},{6,4},{7,5},{8,14},{9,15},{10,... | collective-permute-start | bytes 540680 | tf_op jit(solution)/shard_map/ppermute | solution.py:160
  255.3 4.1 %collective-permute-done.9 = bf16[64,1408]{1,0:T(8,128)(2,1)S(1)} collective-permute-done((bf16[64,1408]{1,0:T(8,128)(2,1)S(1)}, bf16[64,1408]{1,0:T(8,128)(2,1)S(1)}, u32[]{:S(2)}, u32[]{:S(2)}) %collective-permute-start.9) | collective-permute-done | bytes 180256 | tf_op jit(solution)/shard_map/ppermute | solution.py:160
  259.5 4.0 %collective-permute-done.5 = bf16[64,1408]{1,0:T(8,128)(2,1)} collective-permute-done((bf16[64,1408]{1,0:T(8,128)(2,1)S(1)}, bf16[64,1408]{1,0:T(8,128)(2,1)}, u32[]{:S(2)}, u32[]{:S(2)}) %collective-permute-start.5) | collective-permute-done | bytes 180256 | tf_op jit(solution)/shard_map/ppermute | solution.py:160
  263.5 7.6 %collective-permute-done.7 = bf16[64,1408]{1,0:T(8,128)(2,1)} collective-permute-done((bf16[64,1408]{1,0:T(8,128)(2,1)S(1)}, bf16[64,1408]{1,0:T(8,128)(2,1)}, u32[]{:S(2)}, u32[]{:S(2)}) %collective-permute-start.7) | collective-permute-done | bytes 180256 | tf_op jit(solution)/shard_map/ppermute | solution.py:160
  284.6 9.5 %all-to-all-done.6 = bf16[8,64,256]{2,1,0:T(8,128)(2,1)S(1)} async-done(((bf16[8,64,256]{2,1,0:T(8,128)(2,1)}), bf16[8,64,256]{2,1,0:T(8,128)(2,1)S(1)}, u32[]{:S(2)}, u32[]{:S(2)}) %all-to-all-start.6) | async-done | bytes 262176 | tf_op jit(solution)/shard_map/all_to_all | solution.py:36
  295.5 4.2 %all-to-all-start.7 = ((bf16[4,64,2048]{2,1,0:T(8,128)(2,1)}), bf16[4,64,2048]{2,1,0:T(8,128)(2,1)}, u32[]{:S(2)}, u32[]{:S(2)}) async-start(bf16[4,64,2048]{2,1,0:T(8,128)(2,1)} %broadcast_in_dim.130), calls=%async_computation.7 | async-start | bytes 2097152 | tf_op jit(solution)/shard_map/all_to_all | solution.py:36
  301.8 11.5 %all-to-all-done.7 = bf16[4,64,2048]{2,1,0:T(8,128)(2,1)} async-done(((bf16[4,64,2048]{2,1,0:T(8,128)(2,1)}), bf16[4,64,2048]{2,1,0:T(8,128)(2,1)}, u32[]{:S(2)}, u32[]{:S(2)}) %all-to-all-start.7) | async-done | bytes 1048608 | tf_op jit(solution)/shard_map/all_to_all | solution.py:36
  (148 shorter events, 58.5 us)
Async XLA Ops:
  6.5 264.5 %copy-start = (bf16[256,1,1408]{2,0,1:T(8,128)(2,1)S(1)}, bf16[256,1,1408]{2,0,1:T(8,128)(2,1)}, u32[]{:S(2)}) copy-start(bf16[256,1,1408]{2,0,1:T(8,128)(2,1)} %param.35) | copy-start | bytes 2162692
  6.5 61.7 %all-gather.4.cloned.1.call-start = ((), (), s32[]{:S(2)}) async-start(), calls=%async_computation.8 | async-start | bytes 5971968 | tf_op jit(solution)/shard_map/all_gather | solution.py:84
  8.7 149.3 %all-gather.6.cloned.1.call-start = ((), (), s32[]{:S(2)}) async-start(), calls=%async_computation.9 | async-start | bytes 5308416 | tf_op jit(solution)/shard_map/all_gather | solution.py:89
  9.0 59.3 %copy-start.1 = (bf16[1,1024,1152]{2,1,0:T(8,128)(2,1)S(1)}, bf16[1,1024,1152]{2,1,0:T(8,128)(2,1)}, u32[]{:S(2)}) copy-start(bf16[1,1024,1152]{2,1,0:T(8,128)(2,1)} %param.18) | copy-start | bytes 7077892
  81.1 33.1 %all-to-all-start.1 = ((bf16[4,256,1152]{2,1,0:T(8,128)(2,1)}), bf16[4,256,1152]{2,1,0:T(8,128)(2,1)}, u32[]{:S(2)}, u32[]{:S(2)}) async-start(bf16[4,256,1152]{2,1,0:T(8,128)(2,1)} %bitcast.198), calls=%async_computation.1 | async-start | bytes 4718592 | tf_op jit(solution)/shard_map/all_to_all | solution.py:36
  85.7 130.6 %all-gather.8.cloned.1.call-start = ((), (), s32[]{:S(2)}) async-start(), calls=%async_computation.10 | async-start | bytes 9732096 | tf_op jit(solution)/shard_map/all_gather | solution.py:99
  126.5 31.5 %all-to-all-start.2 = ((bf16[4,64,4608]{2,1,0:T(8,128)(2,1)}), bf16[4,64,4608]{2,1,0:T(8,128)(2,1)S(1)}, u32[]{:S(2)}, u32[]{:S(2)}) async-start(bf16[4,64,4608]{2,1,0:T(8,128)(2,1)} %broadcast_in_dim.77), calls=%async_computation.2 | async-start | bytes 4718592 | tf_op jit(solution)/shard_map/all_to_all | solution.py:36
  161.8 18.9 %copy-start.3 = (bf16[4,128,2048]{2,1,0:T(8,128)(2,1)S(1)}, bf16[4,128,2048]{2,1,0:T(8,128)(2,1)}, u32[]{:S(2)}) copy-start(bf16[4,128,2048]{2,1,0:T(8,128)(2,1)} %all_to_all.40) | copy-start | bytes 6291460
  163.0 17.7 %all-to-all-start.3 = ((bf16[4,256,512]{1,2,0:T(8,128)(2,1)}), bf16[4,256,512]{1,2,0:T(8,128)(2,1)}, u32[]{:S(2)}, u32[]{:S(2)}) async-start(bf16[4,256,512]{1,2,0:T(8,128)(2,1)} %broadcast_in_dim.122), calls=%async_computation.3 | async-start | bytes 2097152 | tf_op jit(solution)/shard_map/all_to_all | solution.py:36
  184.5 17.2 %all-to-all-start.4 = ((bf16[8,64,256]{2,1,0:T(8,128)(2,1)}), bf16[8,64,256]{2,1,0:T(8,128)(2,1)S(1)}, u32[]{:S(2)}, u32[]{:S(2)}) async-start(bf16[8,64,256]{2,1,0:T(8,128)(2,1)} %bitcast.191), calls=%async_computation.4 | async-start | bytes 524288 | tf_op jit(solution)/shard_map/all_to_all | solution.py:36
  206.3 3.6 %collective-permute-start = (bf16[256,2816]{1,0:T(8,128)(2,1)}, bf16[256,2816]{1,0:T(8,128)(2,1)}, u32[]{:S(2)}, u32[]{:S(2)}) collective-permute-start(bf16[256,2816]{1,0:T(8,128)(2,1)} %fusion.40), channel_id=1, source_target_pairs={{0,1},{1,0},{2,3},{3,2},{4,5},{5,4},{6,7},{7,6},{8,9},{9,8},{10,11... | collective-permute-start | bytes 4325384 | tf_op jit(solution)/shard_map/ppermute | solution.py:148
  212.4 17.9 %collective-permute-start.1 = (bf16[64,2816]{1,0:T(8,128)(2,1)S(1)}, bf16[64,2816]{1,0:T(8,128)(2,1)S(1)}, u32[]{:S(2)}, u32[]{:S(2)}) collective-permute-start(bf16[64,2816]{1,0:T(8,128)(2,1)S(1)} %get-tuple-element.37), channel_id=1, source_target_pairs={{0,2},{1,3},{2,4},{3,5},{4,6},{5,7},{6,0},{7,1},{8,10},{9,11},{10,... | collective-permute-start | bytes 1081352 | tf_op jit(solution)/shard_map/ppermute | solution.py:154
  213.0 27.3 %collective-permute-start.2 = (bf16[64,2816]{1,0:T(8,128)(2,1)S(1)}, bf16[64,2816]{1,0:T(8,128)(2,1)S(1)}, u32[]{:S(2)}, u32[]{:S(2)}) collective-permute-start(bf16[64,2816]{1,0:T(8,128)(2,1)S(1)} %get-tuple-element.36), channel_id=1, source_target_pairs={{0,4},{1,5},{2,6},{3,7},{4,0},{5,1},{6,2},{7,3},{8,12},{9,13},{10,... | collective-permute-start | bytes 1081352 | tf_op jit(solution)/shard_map/ppermute | solution.py:154
  213.3 27.0 %collective-permute-start.3 = (bf16[64,2816]{1,0:T(8,128)(2,1)S(1)}, bf16[64,2816]{1,0:T(8,128)(2,1)S(1)}, u32[]{:S(2)}, u32[]{:S(2)}) collective-permute-start(bf16[64,2816]{1,0:T(8,128)(2,1)S(1)} %get-tuple-element.35), channel_id=1, source_target_pairs={{0,6},{1,7},{2,0},{3,1},{4,2},{5,3},{6,4},{7,5},{8,14},{9,15},{10,... | collective-permute-start | bytes 1081352 | tf_op jit(solution)/shard_map/ppermute | solution.py:154
  241.1 34.6 %all-to-all-start.5 = ((bf16[4,128,2048]{2,1,0:T(8,128)(2,1)}), bf16[4,128,2048]{2,1,0:T(8,128)(2,1)S(1)}, u32[]{:S(2)}, u32[]{:S(2)}) async-start(bf16[4,128,2048]{2,1,0:T(8,128)(2,1)} %bitcast.200), calls=%async_computation.5 | async-start | bytes 4194304 | tf_op jit(solution)/shard_map/all_to_all | solution.py:36
  246.1 13.3 %collective-permute-start.9 = (bf16[64,1408]{1,0:T(8,128)(2,1)S(1)}, bf16[64,1408]{1,0:T(8,128)(2,1)S(1)}, u32[]{:S(2)}, u32[]{:S(2)}) collective-permute-start(bf16[64,1408]{1,0:T(8,128)(2,1)S(1)} %fusion.78), channel_id=1, source_target_pairs={{0,6},{1,7},{2,0},{3,1},{4,2},{5,3},{6,4},{7,5},{8,14},{9,15},{10,... | collective-permute-start | bytes 540680 | tf_op jit(solution)/shard_map/ppermute | solution.py:160
  253.4 10.1 %collective-permute-start.5 = (bf16[64,1408]{1,0:T(8,128)(2,1)S(1)}, bf16[64,1408]{1,0:T(8,128)(2,1)}, u32[]{:S(2)}, u32[]{:S(2)}) collective-permute-start(bf16[64,1408]{1,0:T(8,128)(2,1)S(1)} %fusion.78), channel_id=1, source_target_pairs={{0,2},{1,3},{2,4},{3,5},{4,6},{5,7},{6,0},{7,1},{8,10},{9,11},{10,... | collective-permute-start | bytes 540680 | tf_op jit(solution)/shard_map/ppermute | solution.py:160
  254.2 16.9 %collective-permute-start.7 = (bf16[64,1408]{1,0:T(8,128)(2,1)S(1)}, bf16[64,1408]{1,0:T(8,128)(2,1)}, u32[]{:S(2)}, u32[]{:S(2)}) collective-permute-start(bf16[64,1408]{1,0:T(8,128)(2,1)S(1)} %fusion.78), channel_id=1, source_target_pairs={{0,4},{1,5},{2,6},{3,7},{4,0},{5,1},{6,2},{7,3},{8,12},{9,13},{10,... | collective-permute-start | bytes 540680 | tf_op jit(solution)/shard_map/ppermute | solution.py:160
  255.3 19.0 %collective-permute-start.4 = (bf16[64,1408]{1,0:T(8,128)(2,1)S(1)}, bf16[64,1408]{1,0:T(8,128)(2,1)S(1)}, u32[]{:S(2)}, u32[]{:S(2)}) collective-permute-start(bf16[64,1408]{1,0:T(8,128)(2,1)S(1)} %fusion.78), channel_id=1, source_target_pairs={{0,1},{1,0},{2,3},{3,2},{4,5},{5,4},{6,7},{7,6},{8,9},{9,8},{10,11... | collective-permute-start | bytes 540680 | tf_op jit(solution)/shard_map/ppermute | solution.py:161
  259.5 14.9 %collective-permute-start.10 = (bf16[64,1408]{1,0:T(8,128)(2,1)S(1)}, bf16[64,1408]{1,0:T(8,128)(2,1)S(1)}, u32[]{:S(2)}, u32[]{:S(2)}) collective-permute-start(bf16[64,1408]{1,0:T(8,128)(2,1)S(1)} %collective-permute-done.9), channel_id=1, source_target_pairs={{0,1},{1,0},{2,3},{3,2},{4,5},{5,4},{6,7},{7,6},{8,9},{9,8},{10,11... | collective-permute-start | bytes 540680 | tf_op jit(solution)/shard_map/ppermute | solution.py:161
  263.5 10.9 %collective-permute-start.6 = (bf16[64,1408]{1,0:T(8,128)(2,1)}, bf16[64,1408]{1,0:T(8,128)(2,1)S(1)}, u32[]{:S(2)}, u32[]{:S(2)}) collective-permute-start(bf16[64,1408]{1,0:T(8,128)(2,1)} %collective-permute-done.5), channel_id=1, source_target_pairs={{0,1},{1,0},{2,3},{3,2},{4,5},{5,4},{6,7},{7,6},{8,9},{9,8},{10,11... | collective-permute-start | bytes 540680 | tf_op jit(solution)/shard_map/ppermute | solution.py:161
  271.1 4.7 %collective-permute-start.8 = (bf16[64,1408]{1,0:T(8,128)(2,1)}, bf16[64,1408]{1,0:T(8,128)(2,1)}, u32[]{:S(2)}, u32[]{:S(2)}) collective-permute-start(bf16[64,1408]{1,0:T(8,128)(2,1)} %collective-permute-done.7), channel_id=1, source_target_pairs={{0,1},{1,0},{2,3},{3,2},{4,5},{5,4},{6,7},{7,6},{8,9},{9,8},{10,11... | collective-permute-start | bytes 540680 | tf_op jit(solution)/shard_map/ppermute | solution.py:161
  281.0 13.2 %all-to-all-start.6 = ((bf16[8,64,256]{2,1,0:T(8,128)(2,1)}), bf16[8,64,256]{2,1,0:T(8,128)(2,1)S(1)}, u32[]{:S(2)}, u32[]{:S(2)}) async-start(bf16[8,64,256]{2,1,0:T(8,128)(2,1)} %bitcast.53), calls=%async_computation.6 | async-start | bytes 524288 | tf_op jit(solution)/shard_map/all_to_all | solution.py:36
  295.5 17.9 %all-to-all-start.7 = ((bf16[4,64,2048]{2,1,0:T(8,128)(2,1)}), bf16[4,64,2048]{2,1,0:T(8,128)(2,1)}, u32[]{:S(2)}, u32[]{:S(2)}) async-start(bf16[4,64,2048]{2,1,0:T(8,128)(2,1)} %broadcast_in_dim.130), calls=%async_computation.7 | async-start | bytes 2097152 | tf_op jit(solution)/shard_map/all_to_all | solution.py:36
  (24 other events, 114.4 us)
Sparse Core Ops, SparseCore 0:
  9.0 59.2 all-gather.3
  69.9 50.5 all-gather.5
  122.0 89.0 all-gather.7
